TPU v7x, 32 devices: a whole 2x2x4 slice. The times are simulated.
32 devices in a mesh: rep: 4 (over z), grp: 8 (over y, x, core).
Axes of the slice: x: 2, y: 2, z: 4, core: 2. Of those that a mesh axis runs over, the one named last changes fastest.
Arguments:
- tokens: bfloat16 [192, 197, 768], P(('rep', 'grp')), may hold values from -6 to 6
- cotangent: bfloat16 [192, 197, 768], P(('rep', 'grp')), may hold values from -6 to 6
- heads_in: bfloat16 [768, 2304], P('grp'), may hold values from -0.3125 to 0.3125
- heads_out: bfloat16 [768, 768], P('grp'), may hold values from -0.875 to 0.875
- slot_router: bfloat16 [768, 4], P('grp'), may hold values from -0.109375 to 0.109375
- first_gain: bfloat16 [768], P('grp'), may hold values from 0.5 to 1.5
- second_gain: bfloat16 [768], P('grp'), may hold values from 0.5 to 1.5
- expert_in: bfloat16 [8, 768, 1536], P('grp'), may hold values from -3 to 3
- expert_out: bfloat16 [8, 1536, 768], P('grp'), may hold values from -0.21875 to 0.21875
Outputs:
- output: bfloat16 [192, 197, 768], P(('rep', 'grp'))
- token_grad: bfloat16 [192, 197, 768], P(('rep', 'grp'))
- heads_in_grad: float32 [768, 2304], P('grp')
- heads_out_grad: float32 [768, 768], P('grp')
- router_grad: float32 [768, 4], P('grp')
- first_gain_grad: float32 [768], P('grp')
- second_gain_grad: float32 [768], P('grp')
- expert_in_grad: float32 [8, 768, 1536], P('grp')
- expert_out_grad: float32 [8, 1536, 768], P('grp')
All inputs are finite; a program needn't handle non-finite values.
Results may differ from a plain program's by a relative error of at most 0.019.
Values may be sent and summed in bfloat16 or wider, within the bound.
No kernel may reach another device: no remote copies, remote signals or barrier semaphores. Data moves between devices by JAX's collectives and lax.ppermute only.
A program may use at most 192 MiB of HBM per device.

v0:
```python
import functools

import jax
import jax.numpy as jnp
from jax import lax
from jax.experimental import pallas as pl
from jax.experimental.pallas import tpu as pltpu
from jax.sharding import PartitionSpec as P

HEADS = 12
LANES = 128
F32 = jnp.float32
BF16 = jnp.bfloat16
LOW = -1e30

NN = (((1,), (0,)), ((), ()))
NT = (((1,), (1,)), ((), ()))
TN = (((0,), (0,)), ((), ()))


def dot(left, right, form=NN):
    return lax.dot_general(left, right, form, preferred_element_type=F32)


def swap(values, axis, size, bit):
    return lax.ppermute(values, axis, [(place, place ^ bit) for place in range(size)])


def after(values, *others):
    return lax.optimization_barrier((values, others))[0]


def gather_first(own):
    return swap(own[0], "grp", 8, 2), swap(own[1], "grp", 8, 4)


def gather_second(joined):
    return swap(joined[0], "grp", 8, 4), swap(joined[1], "grp", 8, 2)


def gather_last(*stages):
    held = tuple(part for stage in stages for part in stage)
    return held + tuple(swap(part, "grp", 8, 1) for part in held)


def as_gathered(blocks, cut):
    held = []
    for k in range(2):
        own, x, y, far = blocks[k], blocks[k + 2], blocks[k + 4], blocks[k + 6]
        held += [own[:cut], own[cut:], x[:cut], y[cut:]]
        held += [jnp.concatenate([y[:cut], far[:cut]]), jnp.concatenate([x[cut:], far[cut:]])]
    return tuple(held)


def iota(shape, axis):
    return lax.broadcasted_iota(jnp.int32, shape, axis)


def normalize(values):
    center = values - jnp.mean(values, axis=-1, keepdims=True)
    factor = lax.rsqrt(jnp.mean(center * center, axis=-1, keepdims=True) + 1e-06)
    return center * factor, factor


def norm_back(scaled, normed, factor):
    inner = (
        scaled
        - jnp.mean(scaled, axis=-1, keepdims=True)
        - normed * jnp.mean(scaled * normed, axis=-1, keepdims=True)
    )
    return factor * inner


def pieces_of(rows, extra):
    half = rows // 2
    cut = extra + half
    for core in range(2):
        base = 6 * core
        yield base, extra, core, 0
        yield base + 1, 0, core, half
        yield base + 2, extra, core + 2, 0
        yield base + 3, 0, core + 4, half
        yield base + 4, extra, core + 4, 0
        yield base + 4, cut + extra, core + 6, 0
        yield base + 5, 0, core + 2, half
        yield base + 5, half, core + 6, half


def place_pieces(order_ref, pieces, rows, extra, target, columns):
    half = rows // 2
    for n, start, block, offset in pieces_of(rows, extra):
        place = pl.multiple_of(order_ref[block] * rows + offset, 16)
        target[pl.ds(place, half), :] = pieces[n][start : start + half, columns]


def store_blocks(order_ref, source, targets, columns):
    rows = source.shape[0] // 8
    n = 0
    for target in targets:
        for k in range(target.shape[0] // rows):
            start = pl.multiple_of(order_ref[8 + n] * rows, 32)
            target[k * rows : (k + 1) * rows, columns] = source[pl.ds(start, rows), :].astype(BF16)
            n += 1


def gather_small(order_ref, pieces, rows, extra, small_ref):
    total = jnp.zeros(small_ref.shape, F32)
    lane = iota((LANES, small_ref.shape[1]), 0)
    place = iota((LANES, small_ref.shape[1]), 1)
    cut = extra + rows // 2
    for core in range(2):
        for n, start, block in ((0, 0, 0), (2, 0, 2), (4, 0, 4), (4, cut, 6)):
            held = pieces[6 * core + n][start : start + extra, :LANES]
            fits = (place == order_ref[block + core] * rows + lane) & (lane < rows)
            total = total + dot(held, jnp.where(fits, 1.0, 0.0).astype(BF16))
    small_ref[...] = total


def rows_of(place, tall):
    return pl.ds(pl.multiple_of(place * tall, 16), tall)


def each_image(images, together, body):
    if images % together:
        together = 1
    if together == images:
        for i in range(images):
            body(i)
        return

    @pl.loop(0, images // together)
    def _(step):
        for k in range(together):
            body(step * together + k)


VM = pl.BlockSpec(memory_space=pltpu.VMEM)
SM = pl.BlockSpec(memory_space=pltpu.SMEM)


def call(body, name, inputs, outputs, scratch, limit, flops, hbm=()):
    return pl.pallas_call(
        body,
        in_specs=[SM if x.dtype == jnp.int32 else VM for x in inputs],
        out_specs=[VM] * len(outputs),
        out_shape=[
            jax.ShapeDtypeStruct(shape, kind) if n in hbm else pltpu.VMEM(shape, kind)
            for n, (shape, kind) in enumerate(outputs)
        ],
        scratch_shapes=[pltpu.VMEM(shape, kind) for shape, kind in scratch],
        compiler_params=pltpu.CompilerParams(vmem_limit_bytes=min(limit, 10) * 1024 * 1024),
        cost_estimate=pl.CostEstimate(flops=int(flops), bytes_accessed=1000000, transcendentals=0),
        name=name,
    )(*inputs)


def prepare_body(in_ref, out_ref, router_ref, one_ref, two_ref, h0, h1, t0, t1):
    rows, features = out_ref.shape
    half = rows // 2
    part = features // 3
    extra = h0.shape[0] - half
    small = [ref[...].astype(F32) for ref in (one_ref, two_ref, router_ref)]
    small.append(jnp.zeros((extra - 2 - router_ref.shape[0], rows), F32))
    small = jnp.concatenate(small, axis=0)
    small = jnp.concatenate([small, jnp.zeros((extra, LANES - rows), F32)], axis=1)
    h0[:extra, :] = jnp.zeros((extra, h0.shape[1]), BF16)
    h0[:extra, :LANES] = small.astype(BF16)
    for head, tail, start, here in ((h0, t0, extra, slice(0, half)), (h1, t1, 0, slice(half, rows))):
        for k in range(3):
            base = k * features
            head[start:, k * part : (k + 1) * part] = in_ref[here, base : base + part]
            tail[:, 2 * k * part : 2 * (k + 1) * part] = in_ref[here, base + part : base + features]
        tail[:, 2 * features :] = out_ref[here, :]


def prepare(heads_in, heads_out, router, one, two):
    rows, features = heads_out.shape
    extra = -(-(router.shape[0] + 2) // 16) * 16
    inputs = (heads_in, heads_out, router, one, two)
    outputs = [
        (extra + rows // 2, features),
        (rows // 2, features),
        (rows // 2, 3 * features),
        (rows // 2, 3 * features),
    ]
    return pl.pallas_call(
        prepare_body,
        grid=(1,),
        in_specs=[pl.BlockSpec(x.shape, lambda i: (0, 0)) for x in inputs],
        out_specs=[VM] * len(outputs),
        out_shape=[pltpu.VMEM(shape, BF16) for shape in outputs],
        compiler_params=pltpu.CompilerParams(vmem_limit_bytes=4 * 1024 * 1024),
        name="prepare",
    )(*inputs)


def join_body(a0, a1, b0, b1, a_ref, b_ref):
    for first, second, target in ((a0, a1, a_ref), (b0, b1, b_ref)):
        target[: first.shape[0], :] = first[...]
        target[first.shape[0] :, :] = second[...]


def join(own, got):
    outputs = [((2 * x.shape[0], x.shape[1]), BF16) for x in own]
    return call(join_body, "join", (own[0], got[0], own[1], got[1]), outputs, [], 4, 1e6)


def attend_body(first, images, places, order_ref, source_ref, *refs):
    pieces, refs = refs[:12], refs[12:]
    features = source_ref.shape[1]
    rows = features // 8
    if first:
        act_ref, small_ref, weight, joint_ref, prob_ref, mixed_ref = refs
        extra = small_ref.shape[0]
    else:
        out_weight, weight, joint_ref, prob_ref, mixed_ref = refs
        act_ref = source_ref
        extra = 0
    tall = source_ref.shape[0] // images
    width = weight.shape[1]
    place_pieces(order_ref, pieces, rows, extra, weight, slice(0, width))
    if first:
        gather_small(order_ref, pieces, rows, extra, small_ref)

        for i in range(images):
            here = rows_of(i, tall)
            normed, _ = normalize(source_ref[here, :].astype(F32))
            act_ref[here, :] = (normed * small_ref[0:1, :]).astype(BF16)
    else:
        place_pieces(order_ref, pieces, rows, 0, out_weight, slice(width, width + features))

    for i in range(images // 2):
        here = rows_of(i, 2 * tall)
        joint_ref[here, :] = dot(act_ref[here, :], weight[...]).astype(BF16)

    third = width // 3
    heads = prob_ref.shape[0] // images
    low = iota((tall, LANES), 1) < LANES // 2
    inside = iota((tall, LANES), 0) < places
    seen = iota((tall, tall), 1) < places

    def attend_image(i):
        here = rows_of(i, tall)
        for pair in range(third // LANES):
            query, keys, values = (
                joint_ref[here, part * third + pair * LANES : part * third + (pair + 1) * LANES]
                for part in range(3)
            )
            query = query * 0.125
            values_ones = jnp.concatenate([values, jnp.ones_like(values)], axis=1)
            outs = []
            for side in range(2):
                mine = low if side == 0 else ~low
                scores = dot(jnp.where(mine, query, 0), keys, NT)
                scores = jnp.where(seen, scores, LOW)
                power = jnp.exp(scores - jnp.max(scores, axis=1, keepdims=True)).astype(BF16)
                got = dot(power, values_ones)
                shrink = 1.0 / got[:, LANES:]
                outs.append(got[:, :LANES] * shrink)
                shrink = jnp.concatenate([shrink, shrink[:, : tall - LANES]], axis=1)
                prob_ref[i * heads + 2 * pair + side] = (power.astype(F32) * shrink).astype(BF16)
            mixed = jnp.where(inside, jnp.where(low, outs[0], outs[1]), 0.0)
            mixed_ref[here, pair * LANES : (pair + 1) * LANES] = mixed.astype(BF16)

    each_image(images, 2, attend_image)


def attend(first, images, places, order, source, pieces, width):
    total, features = source.shape
    tall = total // images
    heads = width // 3 // 64
    extra = pieces[0].shape[0] - features // 16
    outputs = [
        ((features, width), BF16),
        ((total, width), BF16),
        ((images * heads, tall, tall), BF16),
        ((total, width // 3), BF16),
    ]
    if first:
        outputs = [((total, features), BF16), ((extra, features), F32)] + outputs
    else:
        outputs = [((features, features), BF16)] + outputs
    return call(
        functools.partial(attend_body, first, images, places),
        "attend",
        (order, source, *pieces),
        outputs,
        [],
        12,
        2 * total * features * width * 2,
    )


def softmaxes(logits, places, experts):
    rows = iota(logits.shape, 0) < experts
    lanes = iota(logits.shape, 1) < places
    wide = jnp.where(lanes, logits, LOW)
    wide = jnp.exp(wide - jnp.max(wide, axis=1, keepdims=True))
    dispatch = wide / jnp.sum(wide, axis=1, keepdims=True)
    tall = jnp.where(rows, logits, LOW)
    tall = jnp.exp(tall - jnp.max(tall, axis=0, keepdims=True))
    combine = tall / jnp.sum(tall, axis=0, keepdims=True)
    return jnp.where(rows, dispatch, 0.0), combine


def slot_rows_of(experts, order_ref, small_ref, slots):
    rows = small_ref.shape[0]
    slot, row = iota((slots, rows), 0), iota((slots, rows), 1)
    chip = order_ref[order_ref.shape[0] - 1]
    fits = (row == (slot ^ chip) + 2) & (slot < experts)
    return dot(jnp.where(fits, 1.0, 0.0).astype(BF16), small_ref[...].astype(BF16)).astype(BF16)


def pick_rows(shape, wanted):
    row, column = iota(shape, 0), iota(shape, 1)
    return jnp.where(column == wanted(row), 1.0, 0.0).astype(BF16)


def route_body(
    images, places, experts, order_ref, token_ref, cot_ref, m0, m1, weight, small_ref,
    resid_ref, logit_ref, *refs,
):
    out_refs, packed_ref = refs[:-1], refs[-1]
    slots = logit_ref.shape[0] // images
    router = slot_rows_of(experts, order_ref, small_ref, slots)
    tall = token_ref.shape[0] // images
    features = token_ref.shape[1]

    for i in range(images // 2):
        here = rows_of(i, 2 * tall)
        mixed = jnp.concatenate([m0[here, :], m1[here, :]], axis=1)
        resid_ref[here, :] = token_ref[here, :].astype(F32) + dot(mixed, weight[...])

    def route_image(i):
        here = rows_of(i, tall)
        normed, _ = normalize(resid_ref[here, :])
        act = (normed * small_ref[1:2, :]).astype(BF16)
        logits = dot(router, act, NT)
        group = rows_of(i, slots)
        logit_ref[group, :] = logits
        dispatch, combine = softmaxes(logits, places, experts)
        packed_ref[group, :features] = dot(dispatch.astype(BF16), act).astype(BF16)
        packed_ref[group, features:] = dot(combine.astype(BF16), cot_ref[here, :]).astype(BF16)

    each_image(images, 3, route_image)

    high = out_refs[0].shape[0]
    pick = pick_rows(
        (experts * high, images * slots),
        lambda n: jnp.where(n % high < images, n % high * slots + n // high, -1),
    )
    packed = dot(pick, packed_ref[...]).astype(BF16)
    for k, out_ref in enumerate(out_refs):
        out_ref[...] = packed[k * high : (k + 1) * high, :]


def route(images, places, experts, slots, order, tokens, cot, mixed, w, small):
    total, features = tokens.shape
    high = -(-images // 8) * 8
    return call(
        functools.partial(route_body, images, places, experts),
        "route",
        (order, tokens, cot, *mixed, w, small),
        [((total, features), F32), ((images * slots, total // images), F32)]
        + [((high, 2 * features), BF16)] * experts,
        [((images * slots, 2 * features), BF16)],
        10,
        4 * total * features * features,
    )


def gelu_parts(values):
    scale, cubic = 0.7978845608028654, 0.044715
    square = values * values
    bent = jnp.tanh(scale * values * (1.0 + cubic * square))
    half = 0.5 * (1.0 + bent)
    slope = half + 0.5 * values * (1.0 - bent * bent) * scale * (1.0 + 3.0 * cubic * square)
    return values * half, slope


def expert_body(count, images, in_ref, out_ref, *refs):
    sources, (packed_ref, keep_ref, give_ref, rows_ref, back_ref) = refs[:count], refs[count:]
    features = in_ref.shape[0]
    high = sources[0].shape[0]
    for k, source in enumerate(sources):
        rows_ref[k * high : (k + 1) * high, :] = source[...]
    rows, arriving = rows_ref[:, :features], rows_ref[:, features:]
    total = jnp.zeros((rows.shape[0], features), F32)
    grad_total = total
    step = 512
    for start in range(0, in_ref.shape[1], step):
        w_in = in_ref[:, start : start + step]
        w_out = out_ref[start : start + step, :]
        hidden, slope = gelu_parts(dot(rows, w_in))
        grad_pre = (dot(arriving, w_out, NT) * slope).astype(BF16)
        total = total + dot(hidden.astype(BF16), w_out)
        grad_total = grad_total + dot(grad_pre, w_in, NT)
    back_ref[:, :features] = total.astype(BF16)
    back_ref[:, features:] = grad_total.astype(BF16)
    half = keep_ref.shape[0]
    keep_ref[...] = back_ref[:half, :]
    give_ref[...] = back_ref[half:, :]
    pick = pick_rows(
        (packed_ref.shape[0], rows_ref.shape[0]), lambda n: n // images * high + n % images
    )
    packed_ref[...] = dot(pick, rows_ref[...]).astype(BF16)


def expert(images, piece_in, piece_out, sources):
    high, wide = sources[0].shape
    rows = high * len(sources)
    return call(
        functools.partial(expert_body, len(sources), images),
        "expert",
        (piece_in, piece_out, *sources),
        [
            ((images * len(sources), wide), BF16),
            ((rows // 2, wide), BF16),
            ((rows // 2, wide), BF16),
        ],
        [((rows, wide), BF16)] * 2,
        8,
        1e9,
    )


def pair_sum_body(parts, keep_ref, *refs):
    got_refs, out_refs = refs[:parts], refs[parts:]
    rows = out_refs[0].shape[0]
    each = len(out_refs) // parts
    for k, out_ref in enumerate(out_refs):
        kept = keep_ref[k * rows : (k + 1) * rows, :].astype(F32)
        got = got_refs[k // each][k % each * rows : (k % each + 1) * rows, :].astype(F32)
        out_ref[...] = (kept + got).astype(BF16)


def pair_sum(keep, got, count):
    shape = (keep.shape[0] // count, keep.shape[1])
    body = functools.partial(pair_sum_body, len(got))
    return call(body, "pair_sum", (keep, *got), [(shape, BF16)] * count, [], 4, 1e6)


def total_body(*refs):
    refs[-1][...] = sum(ref[...].astype(F32) for ref in refs[:-1]).astype(BF16)


def total_sum(*terms):
    return call(total_body, "total_sum", terms, [(terms[0].shape, BF16)], [], 4, 1e6)[0]


def split_sum_body(order_ref, *refs):
    terms, (mine_ref, give_ref, scratch) = refs[:-3], refs[-3:]
    scratch[...] = sum(ref[...].astype(F32) for ref in terms)
    half = mine_ref.shape[0]
    odd = order_ref[order_ref.shape[0] - 2]
    mine = pl.multiple_of(odd * half, 16)
    other = pl.multiple_of((1 - odd) * half, 16)
    mine_ref[...] = scratch[pl.ds(mine, half), :].astype(BF16)
    give_ref[...] = scratch[pl.ds(other, half), :].astype(BF16)


def split_sum(order, *terms):
    rows, wide = terms[0].shape
    shape = (rows // 2, wide)
    return call(
        split_sum_body, "split_sum", (order, *terms), [(shape, BF16)] * 2, [((rows, wide), F32)], 8, 1e6
    )


def shares_body(
    experts, order_ref, head_ref, head_other, tail_ref, tail_other, w_ref, gain_ref,
    in_ref, out_ref, router_ref, gain_one_ref, gain_two_ref, tail,
):
    rows, features = out_ref.shape
    half = rows // 2
    odd = order_ref[order_ref.shape[0] - 2]
    tail[pl.ds(pl.multiple_of(odd * half, 16), half), :] = tail_ref[...].astype(F32)
    tail[pl.ds(pl.multiple_of((1 - odd) * half, 16), half), :] = tail_other[...].astype(F32)
    part = features // 3
    for k in range(3):
        here = slice(k * part, (k + 1) * part)
        in_ref[:, k * features : k * features + part] = (
            head_ref[:, here].astype(F32) + head_other[:, here].astype(F32)
        )
        in_ref[:, k * features + part : (k + 1) * features] = tail[:, 2 * k * part : 2 * (k + 1) * part]
    out_ref[...] = tail[:, 2 * features : 3 * features]
    rest = tail[:, 3 * features :]
    rest = rest.T
    router_ref[...] = rest[:experts, :]
    gain_two_ref[...] = rest[experts : experts + 1, :]
    gain_one = jnp.sum(in_ref[...] * w_ref[...].astype(F32), axis=1, keepdims=True)
    gain_one = jnp.broadcast_to(gain_one, (rows, LANES)).T[:1, :]
    gain_one_ref[...] = gain_one / gain_ref[...].astype(F32)


def shares(experts, order, head, head_other, tail, tail_other, w, gain):
    rows, features = head.shape
    return call(
        functools.partial(shares_body, experts),
        "shares",
        (order, head, head_other, tail, tail_other, w, gain),
        [
            (w.shape, F32),
            ((rows, features), F32),
            ((experts, rows), F32),
            ((1, rows), F32),
            ((1, rows), F32),
        ],
        [((rows, tail.shape[1]), F32)],
        8,
        1e6,
        hbm=range(5),
    )


def expert_grad_body(count, *refs):
    sources, (in_ref, out_ref, grad_in_ref, grad_out_ref) = refs[:count], refs[count:]
    features = in_ref.shape[0]
    every = jnp.concatenate([source[...] for source in sources], axis=0)
    rows, arriving = every[:, :features], every[:, features:]
    hidden, slope = gelu_parts(dot(rows, in_ref[...]))
    grad_pre = (dot(arriving, out_ref[...], NT) * slope).astype(BF16)
    grad_in_ref[...] = dot(rows, grad_pre, TN)
    grad_out_ref[...] = dot(hidden.astype(BF16), arriving, TN)


def expert_grad(sources, piece_in, piece_out):
    features, hidden = piece_in.shape
    step = 256
    wide = pl.BlockSpec((features, step), lambda i: (0, i))
    high = pl.BlockSpec((step, features), lambda i: (i, 0))
    return pl.pallas_call(
        functools.partial(expert_grad_body, len(sources)),
        grid=(hidden // step,),
        in_specs=[pl.BlockSpec(x.shape, lambda i: (0, 0)) for x in sources] + [wide, high],
        out_specs=[wide, high],
        out_shape=[
            jax.ShapeDtypeStruct(piece_in.shape, F32),
            jax.ShapeDtypeStruct(piece_out.shape, F32),
        ],
        compiler_params=pltpu.CompilerParams(vmem_limit_bytes=16 * 1024 * 1024),
        cost_estimate=pl.CostEstimate(
            flops=1600 * piece_in.size, bytes_accessed=14000000, transcendentals=0
        ),
        name="expert_grad",
    )(*sources, piece_in, piece_out)


def back_body(
    images, places, experts, order_ref, resid_ref, logit_ref, cot_ref, m0, m1, weight, small_ref, *refs
):
    sources, refs = refs[:experts], refs[experts:]
    output_ref, att_ref, grad_mixed_ref, grad_w_ref, grad_side_ref, summed_ref = refs
    slots = logit_ref.shape[0] // images
    router = slot_rows_of(experts, order_ref, small_ref, slots)
    total, features = resid_ref.shape
    tall = total // images
    gain = small_ref[1:2, :]
    high = sources[0].shape[0]
    pick = pick_rows(
        (images * slots, experts * high),
        lambda n: jnp.where(n % slots < experts, n % slots * high + n // slots, -1),
    )
    arrived = jnp.concatenate([source[...] for source in sources], axis=0)
    summed_ref[...] = dot(pick, arrived).astype(BF16)

    def image(i, carry):
        side, gain_sum = carry
        here = rows_of(i, tall)
        group = rows_of(i, slots)
        expert_sum, grad_slots = summed_ref[group, :features], summed_ref[group, features:]
        resid = resid_ref[here, :]
        cot = cot_ref[here, :]
        dispatch, combine = softmaxes(logit_ref[group, :], places, experts)
        output = resid + dot(combine.astype(BF16), expert_sum, TN)
        output_ref[i] = output[:places].astype(BF16)
        normed, factor = normalize(resid)
        act = (normed * gain).astype(BF16)
        grad_comb = dot(expert_sum, cot, NT)
        grad_disp = dot(grad_slots, act, NT)
        grad_logits = combine * (grad_comb - jnp.sum(grad_comb * combine, axis=0, keepdims=True))
        grad_logits = grad_logits + dispatch * (
            grad_disp - jnp.sum(grad_disp * dispatch, axis=1, keepdims=True)
        )
        grad_logits = grad_logits.astype(BF16)
        grad_act = dot(
            jnp.concatenate([dispatch.astype(BF16), grad_logits], axis=0),
            jnp.concatenate([grad_slots, router], axis=0),
            TN,
        )
        att = cot.astype(F32) + norm_back(grad_act * gain, normed, factor)
        att_ref[here, :] = att.astype(BF16)
        return (
            side + dot(grad_logits, act),
            gain_sum + jnp.sum(grad_act * normed, axis=0, keepdims=True),
        )

    together = 3 if images % 3 == 0 else 1

    def some(step, carry):
        for k in range(together):
            carry = image(step * together + k, carry)
        return carry

    carry = (jnp.zeros((slots, features), F32), jnp.zeros((1, features), F32))
    side, gain_sum = lax.fori_loop(0, images // together, some, carry)

    for i in range(images // 2):
        here = rows_of(i, 2 * tall)
        grad_mixed_ref[here, :] = dot(att_ref[here, :], weight[...], NT).astype(BF16)

    part = m0.shape[1]
    grad_w_ref[:part, :] = dot(m0[...], att_ref[...], TN).astype(BF16)
    grad_w_ref[part:, :] = dot(m1[...], att_ref[...], TN).astype(BF16)
    slot = iota((LANES, slots), 0) ^ order_ref[order_ref.shape[0] - 1]
    slot = jnp.where(iota((LANES, slots), 0) < experts, slot, -1)
    fits = jnp.where(slot == iota((LANES, slots), 1), 1.0, 0.0).astype(BF16)
    side = dot(fits, side.astype(BF16))
    side = jnp.where(iota(side.shape, 0) == experts, gain_sum, side)
    grad_side_ref[...] = side.T.astype(BF16)


def back(images, places, experts, order, resid, logits, cot, mixed, w, small, sources):
    total, features = resid.shape
    return call(
        functools.partial(back_body, images, places, experts),
        "back",
        (order, resid, logits, cot, *mixed, w, small, *sources),
        [
            ((images, places, features), BF16),
            ((total, features), BF16),
            ((total, features), BF16),
            ((features, features), BF16),
            ((features, LANES), BF16),
        ],
        [((logits.shape[0], 2 * features), BF16)],
        14,
        8 * total * features * features,
        hbm=(0,),
    )


def attend_back_body(images, extra, offset, order_ref, joint_ref, prob_ref, grad_ref, mixed_ref, act_ref, *refs):
    more, (out_ref, *targets, total) = refs[:extra], refs[extra:]
    width = joint_ref.shape[1]
    tall = joint_ref.shape[0] // images
    third = width // 3
    heads = prob_ref.shape[0] // images
    low = iota((tall, LANES), 1) < LANES // 2

    def back_image(i):
        here = rows_of(i, tall)
        for pair in range(third // LANES):
            query, keys, values = (
                joint_ref[here, part * third + pair * LANES : part * third + (pair + 1) * LANES]
                for part in range(3)
            )
            grad = grad_ref[here, offset + pair * LANES : offset + (pair + 1) * LANES]
            product = grad.astype(F32) * mixed_ref[
                here, pair * LANES : (pair + 1) * LANES
            ].astype(F32)
            query_high, grad_high = query.T, grad.T
            grad_query, grad_keys, grad_values = [], [], []
            for side in range(2):
                mine = low if side == 0 else ~low
                rows = slice(side * LANES // 2, (side + 1) * LANES // 2)
                prob = prob_ref[i * heads + 2 * pair + side]
                inner = jnp.sum(jnp.where(mine, product, 0.0), axis=1, keepdims=True)
                grad_prob = dot(jnp.where(mine, grad, 0), values, NT)
                grad_scores = (prob.astype(F32) * (grad_prob - inner)).astype(BF16)
                grad_query.append(dot(grad_scores, keys))
                grad_keys.append(dot(query_high[rows], grad_scores))
                grad_values.append(dot(grad_high[rows], prob))
            joined = (
                (jnp.where(low, *grad_query) * 0.125).astype(BF16),
                (jnp.concatenate(grad_keys, axis=0) * 0.125).astype(BF16).T,
                jnp.concatenate(grad_values, axis=0).astype(BF16).T,
            )
            for part in range(3):
                out_ref[
                    here, part * third + pair * LANES : part * third + (pair + 1) * LANES
                ] = joined[part]

    each_image(images, 2, back_image)

    step = third
    for start in range(0, width, step):
        total[:, start : start + step] = dot(
            act_ref[...], out_ref[:, start : start + step], TN
        ).astype(BF16)
    store_blocks(order_ref, total, targets, slice(0, width))
    place = width
    for source in more:
        end = place + source.shape[1]
        store_blocks(order_ref, source, targets, slice(place, end))
        place = end


def attend_back(images, offset, order, joint, prob, grad_mixed, mixed, act, splits, more=()):
    total, width = joint.shape
    features = act.shape[1]
    columns = width + sum(m.shape[1] for m in more)
    parts = [((features // n, columns), BF16) for n in splits]
    return call(
        functools.partial(attend_back_body, images, len(more), offset),
        "attend_back",
        (order, joint, prob, grad_mixed, mixed, act, *more),
        [(joint.shape, BF16)] + parts,
        [((features, width), BF16)],
        16,
        2 * total * features * width * 4,
    )


def finish_body(images, places, token_ref, att_ref, j0, j1, s0, s1, small_ref, out_ref):
    total, features = token_ref.shape
    tall = total // images

    @pl.loop(0, images // 2)
    def _(i):
        here = rows_of(i, 2 * tall)
        grad_act = dot(j0[here, :], s0[...], NT) + dot(j1[here, :], s1[...], NT)
        normed, factor = normalize(token_ref[here, :].astype(F32))
        result = att_ref[here, :].astype(F32)
        result = result + norm_back(grad_act * small_ref[0:1, :], normed, factor)
        result = result.astype(BF16)
        out_ref[2 * i] = result[:places]
        out_ref[2 * i + 1] = result[tall : tall + places]


def finish(images, places, tokens, att, joints, weights, small):
    total, features = tokens.shape
    return call(
        functools.partial(finish_body, images, places),
        "finish",
        (tokens, att, *joints, *weights, small),
        [((images, places, features), BF16)],
        [],
        12,
        6 * total * features * features,
        hbm=(0,),
    )[0]


def per_device(
    tokens, cotangent, heads_in, heads_out, slot_router, first_gain, second_gain, expert_in, expert_out
):
    images, places, features = tokens.shape
    experts = slot_router.shape[1]
    group = lax.axis_size("grp")
    reps = lax.axis_size("rep")
    me = lax.axis_index("grp")
    own_rows = heads_in.shape[0]
    chip = me // 2
    odd = lax.axis_index("rep") % 2
    direct = group == 8
    ways = jnp.arange(8, dtype=jnp.int32)
    if direct:
        order = jnp.concatenate([ways ^ me, (ways % 4 * 2 + ways // 4) ^ me, odd[None], chip[None]])
    else:
        order = jnp.concatenate([ways, ways, odd[None], chip[None]])
    tall = -(-places // 16) * 16
    slot_rows = -(-experts // 16) * 16
    part = features // 3
    wide = 3 * part

    grow = ((0, 0), (0, tall - places), (0, 0))
    source = jnp.pad(tokens, grow).reshape(images * tall, features)
    cot = jnp.pad(cotangent, grow).reshape(images * tall, features)
    if direct:
        rows_in, order = lax.optimization_barrier((heads_in, order))
        h0, h1, t0, t1 = prepare(
            rows_in, heads_out, slot_router.T, first_gain[None], second_gain[None]
        )
        head_first = gather_first((h0, h1))
        head_first = after(head_first, source, cot)
        (t0, t1), head_first = lax.optimization_barrier(((t0, t1), head_first))
        head_second = gather_second(join((h0, h1), head_first))
        tail_first = gather_first((t0, t1))
        head = gather_last((h0, h1), head_first, head_second)
        tail_first = after(tail_first, *head)
        tail_join = join((t0, t1), tail_first)
        source = after(source, *tail_join)
    else:
        thirds = [heads_in[:, k * features : (k + 1) * features] for k in range(3)]
        head_part = jnp.concatenate([t[:, :part] for t in thirds], axis=1)
        tail_part = jnp.concatenate([t[:, part:] for t in thirds] + [heads_out], axis=1)
        small = jnp.concatenate([first_gain[None], second_gain[None], slot_router.T], axis=0)
        extra = -(-small.shape[0] // 16) * 16
        head_part = lax.all_gather(head_part, "grp", axis=0, tiled=True).reshape(8, -1, wide)
        small = lax.all_gather(small, "grp", axis=1, tiled=True).reshape(-1, 8, features // 8)
        small = small.transpose(1, 0, 2)
        small = jnp.pad(small, ((0, 0), (0, extra - small.shape[1]), (0, wide - small.shape[2])))
        head = as_gathered(jnp.concatenate([small, head_part], axis=1), extra + features // 16)
        tail_part = lax.all_gather(tail_part, "grp", axis=0, tiled=True)
        tail = as_gathered(tail_part.reshape(8, -1, 3 * features), features // 16)

    act, small, w_head, joint_head, prob_head, mixed_head = attend(
        True, images, places, order, source, head, wide
    )
    if direct:
        tail_second = after(gather_second(tail_join), mixed_head)
        tail = gather_last((t0, t1), tail_first, tail_second)
    w_out, w_tail, joint_tail, prob_tail, mixed_tail = attend(
        False, images, places, order, act, tail, 2 * wide
    )
    mixes = [mixed_head, mixed_tail]
    resid, logits, *leaving = route(
        images, places, experts, slot_rows, order, source, cot, mixes, w_out, small
    )

    arrived = [leaving[0]] + [swap(leaving[k], "grp", group, 2 * k) for k in range(1, experts)]
    arrived = arrived + [swap(part, "grp", group, 1) for part in arrived]
    piece_in, piece_out = expert_in[0], expert_out[0]
    received, kept, given = expert(images, piece_in, piece_out, arrived)
    both = pair_sum(kept, [swap(given, "grp", group, 1)], experts)
    summed = [both[0]] + [swap(both[k], "grp", group, 2 * k) for k in range(1, experts)]
    received = after(received, *summed)
    far = [swap(received, "rep", reps, k) for k in range(1, reps)]
    output, att, grad_mixed, grad_out, grad_side = back(
        images, places, experts, order, resid, logits, cot, mixes, w_out, small, summed
    )
    grad_mixed, far = lax.optimization_barrier((grad_mixed, far))
    grad_joint_tail, keep_tail, give_tail = attend_back(
        images, part, order, joint_tail, prob_tail, grad_mixed, mixed_tail, act, (2, 2), (grad_out, grad_side)
    )
    if direct:
        sums = pair_sum(keep_tail, [swap(give_tail, "grp", group, 1)], 4)
        others = [swap(sums[k], "grp", group, 2 * k) for k in range(1, 4)]
        grad_mixed = after(grad_mixed, *sums)
    grad_joint_head, keep_head, *give_head = attend_back(
        images, 0, order, joint_head, prob_head, grad_mixed, mixed_head, act, (2, 4, 4)
    )
    joints, weights = [grad_joint_head, grad_joint_tail], [w_head, w_tail]
    every = [received] + far
    if direct:
        got = [swap(part, "grp", group, 1) for part in give_head]
        own, others = after((sums[0], others), got)
        mine, give = split_sum(order, own, *others)
        other = swap(give, "rep", reps, 1)
        sums = pair_sum(keep_head, got, 4)
        others = [swap(sums[k], "grp", group, 2 * k) for k in range(1, 4)]
        att = after(att, mine, *sums)
        token_grad = finish(images, places, source, att, joints, weights, small)
        own, others, other = after((sums[0], others, other), token_grad)
        tail_sum = total_sum(mine, other)
        head_sum = total_sum(own, *others)
        every, tail_sum, head_sum = after((every, tail_sum, head_sum), token_grad)
        tail_other = swap(tail_sum, "rep", reps, 2)
        head_other = swap(head_sum, "rep", reps, 1)
        expert_in_grad, expert_out_grad = expert_grad(every, piece_in, piece_out)
        tail_other, head_other = after((tail_other, head_other), expert_in_grad)
        tail_sum, head_sum = total_sum(tail_sum, tail_other), total_sum(head_sum, head_other)
        tail_other = swap(tail_sum, "rep", reps, 1)
        head_other = swap(head_sum, "rep", reps, 3)
        heads_in_grad, heads_out_grad, router_grad, gain_one_grad, gain_two_grad = shares(
            experts, order, head_sum, head_other, tail_sum, tail_other, heads_in, first_gain[None]
        )
        gain_one_grad, gain_two_grad = gain_one_grad[0], gain_two_grad[0]
        router_grad = router_grad.T
    else:
        token_grad = finish(images, places, source, att, joints, weights, small)
        expert_in_grad, expert_out_grad = expert_grad(every, piece_in, piece_out)
        tail_sum = jnp.concatenate([keep_tail, give_tail])
        tail_sum = lax.psum_scatter(tail_sum, "grp", scatter_dimension=0, tiled=True)
        head_sum = jnp.concatenate([keep_head, *give_head])
        head_sum = lax.psum_scatter(head_sum, "grp", scatter_dimension=0, tiled=True)
        tail_sum = lax.psum(tail_sum, "rep").astype(F32)
        head_sum = lax.psum(head_sum, "rep").astype(F32)
        columns = []
        for k in range(3):
            columns.append(head_sum[:, k * part : (k + 1) * part])
            columns.append(tail_sum[:, 2 * k * part : 2 * (k + 1) * part])
        heads_in_grad = jnp.concatenate(columns, axis=1)
        gain_one_grad = jnp.sum(heads_in_grad * heads_in.astype(F32), axis=1)
        gain_one_grad = gain_one_grad / first_gain.astype(F32)
        heads_out_grad, rest = tail_sum[:, 2 * wide : 3 * wide], tail_sum[:, 3 * wide :]
        router_grad, gain_two_grad = rest[:, :experts], rest[:, experts]
    return (
        output,
        token_grad,
        heads_in_grad,
        heads_out_grad,
        router_grad,
        gain_one_grad,
        gain_two_grad,
        expert_in_grad[None],
        expert_out_grad[None],
    )


def solution(mesh):
    token_spec = P(("rep", "grp"), None, None)
    matrix, vector, stack = P("grp", None), P("grp"), P("grp", None, None)
    return jax.shard_map(
        per_device,
        mesh=mesh,
        in_specs=(token_spec, token_spec, matrix, matrix, matrix, vector, vector, stack, stack),
        out_specs=(token_spec, token_spec, matrix, matrix, matrix, vector, vector, stack, stack),
        check_vma=False,
    )
```

profile of v0, /device:TPU:0, one launch (start us, length us, event | category | flops | bytes accessed | tf_op | source)
XLA Modules:
  0.0 168.5 jit_solution(6236524803158532417)
XLA Ops:
  4.7 3.0 %collective-permute-start = (bf16[64,768]{1,0:T(8,128)(2,1)S(1)}, bf16[64,768]{1,0:T(8,128)(2,1)S(1)}, u32[]{:S(2)}, u32[]{:S(2)}) collective-permute-start(bf16[64,768]{1,0:T(8,128)(2,1)S(1)} %get-tuple-element.111.a0.refs_0_), channel_id=1, source_target_pairs={{0,2},{1,3},{2,0},{3,1},{4,6},{5,7},{6,4},{7,5},{8,10},{9,11},{10,... | collective-permute-start | bytes 294920 | tf_op jit(solution)/shard_map/ppermute | solution.py:26
  18.4 2.0 %collective-permute-done.5.refs_5_ = bf16[96,768]{1,0:T(8,128)(2,1)S(1)} collective-permute-done((bf16[96,768]{1,0:T(8,128)(2,1)S(1)}, bf16[96,768]{1,0:T(8,128)(2,1)S(1)}, u32[]{:S(2)}, u32[]{:S(2)}) %collective-permute-start.5) | collective-permute-done | bytes 147488 | tf_op jit(solution)/shard_map/ppermute | solution.py:26
  21.9 2.8 %collective-permute-done.2.a1.refs_2_ = bf16[48,2304]{1,0:T(8,128)(2,1)S(1)} collective-permute-done((bf16[48,2304]{1,0:T(8,128)(2,1)S(1)}, bf16[48,2304]{1,0:T(8,128)(2,1)S(1)}, u32[]{:S(2)}, u32[]{:S(2)}) %collective-permute-start.2) | collective-permute-done | bytes 221216 | tf_op jit(solution)/shard_map/ppermute | solution.py:26
  25.7 6.6 %attend.2 = (bf16[1248,768]{1,0:T(8,128)(2,1)S(1)}, f32[16,768]{1,0:T(8,128)S(1)}, bf16[768,768]{1,0:T(8,128)(2,1)S(1)}, bf16[1248,768]{1,0:T(8,128)(2,1)S(1)}, ...) custom-call(s32[18]{0:T(128)S(1)} %pad_add_fusion.order_ref, bf16[1248,768]{1,0:T(8,128)(2,1)S(1)} %bitcast.18, ...), custom_call_target="tpu_custom_call" | custom-call | flops 2944401408 | bytes 1000000 | tf_op jit(solution)/shard_map/attend/pallas_call | solution.py:142
  32.3 4.4 %collective-permute-done.12.refs_4_ = bf16[96,2304]{1,0:T(8,128)(2,1)S(1)} collective-permute-done((bf16[96,2304]{1,0:T(8,128)(2,1)S(1)}, bf16[96,2304]{1,0:T(8,128)(2,1)S(1)}, u32[]{:S(2)}, u32[]{:S(2)}) %collective-permute-start.12) | collective-permute-done | bytes 442400 | tf_op jit(solution)/shard_map/ppermute | solution.py:26
  40.3 9.0 %attend.3 = (bf16[768,768]{1,0:T(8,128)(2,1)S(1)}, bf16[768,1536]{1,0:T(8,128)(2,1)S(1)}, bf16[1248,1536]{1,0:T(8,128)(2,1)S(1)}, bf16[48,208,208]{2,1,0:T(8,128)(2,1)S(1)}, bf16[1248,512]{1,0:T(8,128)(2,1)S(1)}) custom-call(s32[18]{0:T(128)S(1)} %pad_add_fusion.order_ref, bf16[1248,768]{1,0:T(8,128)(2,1)S(1)} %get-tuple-element.127.source_ref.act_ref, ...), custom_call_target="tpu_custom_call" | custom-call | flops 5888802816 | bytes 1000000 | tf_op jit(solution)/shard_map/attend/pallas_call | solution.py:142
  49.3 5.1 %route.1 = (f32[1248,768]{1,0:T(8,128)S(1)}, f32[96,208]{1,0:T(8,128)S(1)}, bf16[8,1536]{1,0:T(8,128)(2,1)S(1)}, bf16[8,1536]{1,0:T(8,128)(2,1)S(1)}, bf16[8,153...) custom-call(s32[18]{0:T(128)S(1)} %pad_add_fusion.order_ref, bf16[1248,768]{1,0:T(8,128)(2,1)S(1)} %bitcast.19, ...), custom_call_target="tpu_custom_call" | custom-call | flops 2944401408 | bytes 1000000 | tf_op jit(solution)/shard_map/route/pallas_call | solution.py:142
  58.8 2.4 %collective-permute-done.22.refs_3_ = bf16[8,1536]{1,0:T(8,128)(2,1)S(1)} collective-permute-done((bf16[8,1536]{1,0:T(8,128)(2,1)S(1)}, bf16[8,1536]{1,0:T(8,128)(2,1)S(1)}, u32[]{:S(2)}, u32[]{:S(2)}) %collective-permute-start.22) | collective-permute-done | bytes 24608 | tf_op jit(solution)/shard_map/ppermute | solution.py:26
  62.5 2.4 %expert.1 = (bf16[48,1536]{1,0:T(8,128)(2,1)S(1)}, bf16[32,1536]{1,0:T(8,128)(2,1)S(1)}, bf16[32,1536]{1,0:T(8,128)(2,1)S(1)}) custom-call(bf16[768,1536]{1,0:T(8,128)(2,1)S(1)} %bitcast.14, bf16[1536,768]{1,0:T(8,128)(2,1)S(1)} %bitcast.16, bf16[8,1536]{1,0:T(8,128)(2,1)S(1)} %get-tuple-element.135.refs_0_, ...), custom_call_target="tpu_custom_call" | custom-call | flops 1000000000 | bytes 1000000 | tf_op jit(solution)/shard_map/expert/pallas_call | solution.py:142
  70.2 1.8 %collective-permute-done.29.refs_2_ = bf16[8,1536]{1,0:T(8,128)(2,1)S(1)} collective-permute-done((bf16[8,1536]{1,0:T(8,128)(2,1)S(1)}, bf16[8,1536]{1,0:T(8,128)(2,1)S(1)}, u32[]{:S(2)}, u32[]{:S(2)}) %collective-permute-start.29) | collective-permute-done | bytes 24608 | tf_op jit(solution)/shard_map/ppermute | solution.py:26
  73.1 3.6 %collective-permute-start.33 = (bf16[48,1536]{1,0:T(8,128)(2,1)S(1)}, bf16[48,1536]{1,0:T(8,128)(2,1)S(1)}, u32[]{:S(2)}, u32[]{:S(2)}) collective-permute-start(bf16[48,1536]{1,0:T(8,128)(2,1)S(1)} %get-tuple-element.192.refs_0_), channel_id=1, source_target_pairs={{0,24},{8,16},{16,8},{24,0},{1,25},{9,17},{17,9},{25,1},{2,26},{10... | collective-permute-start | bytes 442376 | tf_op jit(solution)/shard_map/ppermute | solution.py:26
  77.5 11.1 %back.1 = (bf16[6,197,768]{2,1,0:T(8,128)(2,1)}, bf16[1248,768]{1,0:T(8,128)(2,1)S(1)}, bf16[1248,768]{1,0:T(8,128)(2,1)S(1)}, bf16[768,768]{1,0:T(8,128)(2,1)S(1)}, bf16[768,128]{1,0:T(8,128)(2,1)S(1)}) custom-call(s32[18]{0:T(128)S(1)} %pad_add_fusion.order_ref, f32[1248,768]{1,0:T(8,128)S(1)} %get-tuple-element.133.resid_ref, ...), custom_call_target="tpu_custom_call" | custom-call | flops 5888802816 | bytes 1000000 | tf_op jit(solution)/shard_map/back/pallas_call | solution.py:142
  88.6 16.0 %attend_back.2 = (bf16[1248,1536]{1,0:T(8,128)(2,1)S(1)}, bf16[384,2432]{1,0:T(8,128)(2,1)S(1)}, bf16[384,2432]{1,0:T(8,128)(2,1)S(1)}) custom-call(s32[18]{0:T(128)S(1)} %pad_add_fusion.order_ref, bf16[1248,1536]{1,0:T(8,128)(2,1)S(1)} %get-tuple-element.147.joint_ref, bf16[48,208,208]{2,1,0:T(8,128)(2,1)S(1)} %get-tuple-element.148.prob_ref, ...), custom_call_target="tpu_custom_call" | custom-call | flops 11777605632 | bytes 1000000 | tf_op jit(solution)/shard_map/attend_back/pallas_call | solution.py:142
  104.7 3.8 %collective-permute-done.34.refs_0_ = bf16[384,2432]{1,0:T(8,128)(2,1)S(1)} collective-permute-done((bf16[384,2432]{1,0:T(8,128)(2,1)S(1)}, bf16[384,2432]{1,0:T(8,128)(2,1)S(1)}, u32[]{:S(2)}, u32[]{:S(2)}) %collective-permute-start.34) | collective-permute-done | bytes 1867808 | tf_op jit(solution)/shard_map/ppermute | solution.py:26
  112.5 8.9 %attend_back.3 = (bf16[1248,768]{1,0:T(8,128)(2,1)S(1)}, bf16[384,768]{1,0:T(8,128)(2,1)S(1)}, bf16[192,768]{1,0:T(8,128)(2,1)S(1)}, bf16[192,768]{1,0:T(8,128)(2,1)S(1)}) custom-call(s32[18]{0:T(128)S(1)} %pad_add_fusion.order_ref, bf16[1248,768]{1,0:T(8,128)(2,1)S(1)} %get-tuple-element.161.joint_ref, ...), custom_call_target="tpu_custom_call" | custom-call | flops 5888802816 | bytes 1000000 | tf_op jit(solution)/shard_map/attend_back/pallas_call | solution.py:142
  127.2 3.2 %collective-permute-done.36.refs_2_ = bf16[96,2432]{1,0:T(8,128)(2,1)S(1)} collective-permute-done((bf16[96,2432]{1,0:T(8,128)(2,1)S(1)}, bf16[96,2432]{1,0:T(8,128)(2,1)S(1)}, u32[]{:S(2)}, u32[]{:S(2)}) %collective-permute-start.36) | collective-permute-done | bytes 466976 | tf_op jit(solution)/shard_map/ppermute | solution.py:26
  130.4 3.2 %collective-permute-done.37.refs_3_ = bf16[96,2432]{1,0:T(8,128)(2,1)S(1)} collective-permute-done((bf16[96,2432]{1,0:T(8,128)(2,1)S(1)}, bf16[96,2432]{1,0:T(8,128)(2,1)S(1)}, u32[]{:S(2)}, u32[]{:S(2)}) %collective-permute-start.37) | collective-permute-done | bytes 466976 | tf_op jit(solution)/shard_map/ppermute | solution.py:26
  135.9 7.8 %finish.1 = bf16[6,197,768]{2,1,0:T(8,128)(2,1)} custom-call(bf16[1248,768]{1,0:T(8,128)(2,1)S(1)} %bitcast.20, bf16[1248,768]{1,0:T(8,128)(2,1)S(1)} %get-tuple-element.176.att_ref, bf16[1248,768]{1,0:T(8,128)(2,1)S(1)} %get-tuple-element.177.j0, bf16[1248,1536]{1,0:T(8,128)(2,1)S(1)} %get-tuple-element.178.j1, bf16[768,768]{1,0:T(8,128)(2,1)S(1)} %get-tuple-element.179.s0, ...), custom_call_target="tpu_custom_call" | custom-call | flops 4416602112 | bytes 1000000 | tf_op jit(solution)/shard_map/finish/pallas_call | solution.py:142
  143.9 3.0 %collective-permute-start.44 = (bf16[48,2432]{1,0:T(8,128)(2,1)S(1)}, bf16[48,2432]{1,0:T(8,128)(2,1)S(1)}, u32[]{:S(2)}, u32[]{:S(2)}) collective-permute-start(bf16[48,2432]{1,0:T(8,128)(2,1)S(1)} %total_sum.4.refs_0_), channel_id=1, source_target_pairs={{0,16},{8,24},{16,0},{24,8},{1,17},{9,25},{17,1},{25,9},{2,18},{10... | collective-permute-start | bytes 700424 | tf_op jit(solution)/shard_map/ppermute | solution.py:26
  146.9 6.7 %expert_grad.1 = (f32[768,1536]{1,0:T(8,128)}, f32[1536,768]{1,0:T(8,128)}) custom-call(bf16[48,1536]{1,0:T(8,128)(2,1)S(1)} %get-tuple-element.192.refs_0_, bf16[48,1536]{1,0:T(8,128)(2,1)S(1)} %collective-permute-done.31.refs_1_, bf16[48,1536]{1,0:T(8,128)(2,1)S(1)} %collective-permute-done.32.refs_2_, ...), custom_call_target="tpu_custom_call" | custom-call | flops 1887436800 | bytes 14000000 | tf_op jit(solution)/shard_map/expert_grad/pallas_call | solution.py:532
  153.5 2.4 %collective-permute-done.44.refs_1_ = bf16[48,2432]{1,0:T(8,128)(2,1)S(1)} collective-permute-done((bf16[48,2432]{1,0:T(8,128)(2,1)S(1)}, bf16[48,2432]{1,0:T(8,128)(2,1)S(1)}, u32[]{:S(2)}, u32[]{:S(2)}) %collective-permute-start.44) | collective-permute-done | bytes 233504 | tf_op jit(solution)/shard_map/ppermute | solution.py:26
  156.1 2.5 %collective-permute-start.46 = (bf16[96,768]{1,0:T(8,128)(2,1)S(1)}, bf16[96,768]{1,0:T(8,128)(2,1)S(1)}, u32[]{:S(2)}, u32[]{:S(2)}) collective-permute-start(bf16[96,768]{1,0:T(8,128)(2,1)S(1)} %total_sum.6.head_ref), channel_id=1, source_target_pairs={{0,24},{8,16},{16,8},{24,0},{1,25},{9,17},{17,9},{25,1},{2,26},{10... | collective-permute-start | bytes 442376 | tf_op jit(solution)/shard_map/ppermute | solution.py:26
  158.6 7.8 %collective-permute-done.46.head_other = bf16[96,768]{1,0:T(8,128)(2,1)S(1)} collective-permute-done((bf16[96,768]{1,0:T(8,128)(2,1)S(1)}, bf16[96,768]{1,0:T(8,128)(2,1)S(1)}, u32[]{:S(2)}, u32[]{:S(2)}) %collective-permute-start.46) | collective-permute-done | bytes 147488 | tf_op jit(solution)/shard_map/ppermute | solution.py:26
  166.8 1.7 %shares.1 = (f32[96,2304]{1,0:T(8,128)}, f32[96,768]{1,0:T(8,128)}, f32[4,96]{1,0:T(4,128)}, f32[1,96]{1,0:T(1,128)}, f32[1,96]{1,0:T(1,128)}) custom-call(s32[18]{0:T(128)S(1)} %pad_add_fusion.order_ref, bf16[96,768]{1,0:T(8,128)(2,1)S(1)} %total_sum.6.head_ref, bf16[96,768]{1,0:T(8,128)(2,1)S(1)} %collective-permute-done.46.head_other, ...), custom_call_target="tpu_custom_call" | custom-call | flops 1000000 | bytes 1000000 | tf_op jit(solution)/shard_map/shares/pallas_call | solution.py:142
  (117 shorter events, 46.3 us)
Async XLA Ops:
  4.7 7.4 %collective-permute-start = (bf16[64,768]{1,0:T(8,128)(2,1)S(1)}, bf16[64,768]{1,0:T(8,128)(2,1)S(1)}, u32[]{:S(2)}, u32[]{:S(2)}) collective-permute-start(bf16[64,768]{1,0:T(8,128)(2,1)S(1)} %get-tuple-element.111.a0.refs_0_), channel_id=1, source_target_pairs={{0,2},{1,3},{2,0},{3,1},{4,6},{5,7},{6,4},{7,5},{8,10},{9,11},{10,... | collective-permute-start | bytes 294920 | tf_op jit(solution)/shard_map/ppermute | solution.py:26
  12.1 5.7 %collective-permute-start.4 = (bf16[128,768]{1,0:T(8,128)(2,1)S(1)}, bf16[128,768]{1,0:T(8,128)(2,1)S(1)}, u32[]{:S(2)}, u32[]{:S(2)}) collective-permute-start(bf16[128,768]{1,0:T(8,128)(2,1)S(1)} %get-tuple-element.119), channel_id=1, source_target_pairs={{0,4},{1,5},{2,6},{3,7},{4,0},{5,1},{6,2},{7,3},{8,12},{9,13},{10,... | collective-permute-start | bytes 589832 | tf_op jit(solution)/shard_map/ppermute | solution.py:26
  13.7 6.6 %collective-permute-start.5 = (bf16[96,768]{1,0:T(8,128)(2,1)S(1)}, bf16[96,768]{1,0:T(8,128)(2,1)S(1)}, u32[]{:S(2)}, u32[]{:S(2)}) collective-permute-start(bf16[96,768]{1,0:T(8,128)(2,1)S(1)} %get-tuple-element.120), channel_id=1, source_target_pairs={{0,2},{1,3},{2,0},{3,1},{4,6},{5,7},{6,4},{7,5},{8,10},{9,11},{10,... | collective-permute-start | bytes 442376 | tf_op jit(solution)/shard_map/ppermute | solution.py:26
  14.5 10.2 %collective-permute-start.2 = (bf16[48,2304]{1,0:T(8,128)(2,1)S(1)}, bf16[48,2304]{1,0:T(8,128)(2,1)S(1)}, u32[]{:S(2)}, u32[]{:S(2)}) collective-permute-start(bf16[48,2304]{1,0:T(8,128)(2,1)S(1)} %get-tuple-element.115.a0.refs_0_), channel_id=1, source_target_pairs={{0,2},{1,3},{2,0},{3,1},{4,6},{5,7},{6,4},{7,5},{8,10},{9,11},{10,... | collective-permute-start | bytes 663560 | tf_op jit(solution)/shard_map/ppermute | solution.py:26
  16.0 8.7 %collective-permute-start.3 = (bf16[48,2304]{1,0:T(8,128)(2,1)S(1)}, bf16[48,2304]{1,0:T(8,128)(2,1)S(1)}, u32[]{:S(2)}, u32[]{:S(2)}) collective-permute-start(bf16[48,2304]{1,0:T(8,128)(2,1)S(1)} %get-tuple-element.116.b0.refs_1_), channel_id=1, source_target_pairs={{0,4},{1,5},{2,6},{3,7},{4,0},{5,1},{6,2},{7,3},{8,12},{9,13},{10,... | collective-permute-start | bytes 663560 | tf_op jit(solution)/shard_map/ppermute | solution.py:26
  17.9 6.9 %collective-permute-start.10 = (bf16[128,768]{1,0:T(8,128)(2,1)S(1)}, bf16[128,768]{1,0:T(8,128)(2,1)S(1)}, u32[]{:S(2)}, u32[]{:S(2)}) collective-permute-start(bf16[128,768]{1,0:T(8,128)(2,1)S(1)} %collective-permute-done.4.refs_4_), channel_id=1, source_target_pairs={{0,1},{1,0},{2,3},{3,2},{4,5},{5,4},{6,7},{7,6},{8,9},{9,8},{10,11... | collective-permute-start | bytes 589832 | tf_op jit(solution)/shard_map/ppermute | solution.py:26
  24.8 11.9 %collective-permute-start.12 = (bf16[96,2304]{1,0:T(8,128)(2,1)S(1)}, bf16[96,2304]{1,0:T(8,128)(2,1)S(1)}, u32[]{:S(2)}, u32[]{:S(2)}) collective-permute-start(bf16[96,2304]{1,0:T(8,128)(2,1)S(1)} %get-tuple-element.123), channel_id=1, source_target_pairs={{0,4},{1,5},{2,6},{3,7},{4,0},{5,1},{6,2},{7,3},{8,12},{9,13},{10,... | collective-permute-start | bytes 1327112 | tf_op jit(solution)/shard_map/ppermute | solution.py:26
  25.4 11.5 %collective-permute-start.13 = (bf16[96,2304]{1,0:T(8,128)(2,1)S(1)}, bf16[96,2304]{1,0:T(8,128)(2,1)S(1)}, u32[]{:S(2)}, u32[]{:S(2)}) collective-permute-start(bf16[96,2304]{1,0:T(8,128)(2,1)S(1)} %get-tuple-element.124), channel_id=1, source_target_pairs={{0,2},{1,3},{2,0},{3,1},{4,6},{5,7},{6,4},{7,5},{8,10},{9,11},{10,... | collective-permute-start | bytes 1327112 | tf_op jit(solution)/shard_map/ppermute | solution.py:26
  25.7 12.3 %collective-permute-start.14 = (bf16[48,2304]{1,0:T(8,128)(2,1)S(1)}, bf16[48,2304]{1,0:T(8,128)(2,1)S(1)}, u32[]{:S(2)}, u32[]{:S(2)}) collective-permute-start(bf16[48,2304]{1,0:T(8,128)(2,1)S(1)} %get-tuple-element.115.a0.refs_0_), channel_id=1, source_target_pairs={{0,1},{1,0},{2,3},{3,2},{4,5},{5,4},{6,7},{7,6},{8,9},{9,8},{10,11... | collective-permute-start | bytes 663560 | tf_op jit(solution)/shard_map/ppermute | solution.py:26
  56.5 4.7 %collective-permute-start.22 = (bf16[8,1536]{1,0:T(8,128)(2,1)S(1)}, bf16[8,1536]{1,0:T(8,128)(2,1)S(1)}, u32[]{:S(2)}, u32[]{:S(2)}) collective-permute-start(bf16[8,1536]{1,0:T(8,128)(2,1)S(1)} %get-tuple-element.138), channel_id=1, source_target_pairs={{0,6},{1,7},{2,4},{3,5},{4,2},{5,3},{6,0},{7,1},{8,14},{9,15},{10,... | collective-permute-start | bytes 73736 | tf_op jit(solution)/shard_map/ppermute | solution.py:26
  73.1 15.5 %collective-permute-start.33 = (bf16[48,1536]{1,0:T(8,128)(2,1)S(1)}, bf16[48,1536]{1,0:T(8,128)(2,1)S(1)}, u32[]{:S(2)}, u32[]{:S(2)}) collective-permute-start(bf16[48,1536]{1,0:T(8,128)(2,1)S(1)} %get-tuple-element.192.refs_0_), channel_id=1, source_target_pairs={{0,24},{8,16},{16,8},{24,0},{1,25},{9,17},{17,9},{25,1},{2,26},{10... | collective-permute-start | bytes 442376 | tf_op jit(solution)/shard_map/ppermute | solution.py:26
  76.7 11.9 %collective-permute-start.32 = (bf16[48,1536]{1,0:T(8,128)(2,1)S(1)}, bf16[48,1536]{1,0:T(8,128)(2,1)S(1)}, u32[]{:S(2)}, u32[]{:S(2)}) collective-permute-start(bf16[48,1536]{1,0:T(8,128)(2,1)S(1)} %get-tuple-element.192.refs_0_), channel_id=1, source_target_pairs={{0,16},{8,24},{16,0},{24,8},{1,17},{9,25},{17,1},{25,9},{2,18},{10... | collective-permute-start | bytes 442376 | tf_op jit(solution)/shard_map/ppermute | solution.py:26
  76.7 11.9 %collective-permute-start.31 = (bf16[48,1536]{1,0:T(8,128)(2,1)S(1)}, bf16[48,1536]{1,0:T(8,128)(2,1)S(1)}, u32[]{:S(2)}, u32[]{:S(2)}) collective-permute-start(bf16[48,1536]{1,0:T(8,128)(2,1)S(1)} %get-tuple-element.192.refs_0_), channel_id=1, source_target_pairs={{0,8},{8,0},{16,24},{24,16},{1,9},{9,1},{17,25},{25,17},{2,10},{10... | collective-permute-start | bytes 442376 | tf_op jit(solution)/shard_map/ppermute | solution.py:26
  109.0 16.8 %collective-permute-start.35 = (bf16[96,2432]{1,0:T(8,128)(2,1)S(1)}, bf16[96,2432]{1,0:T(8,128)(2,1)S(1)}, u32[]{:S(2)}, u32[]{:S(2)}) collective-permute-start(bf16[96,2432]{1,0:T(8,128)(2,1)S(1)} %get-tuple-element.158), channel_id=1, source_target_pairs={{0,2},{1,3},{2,0},{3,1},{4,6},{5,7},{6,4},{7,5},{8,10},{9,11},{10,... | collective-permute-start | bytes 1400840 | tf_op jit(solution)/shard_map/ppermute | solution.py:26
  109.4 21.0 %collective-permute-start.36 = (bf16[96,2432]{1,0:T(8,128)(2,1)S(1)}, bf16[96,2432]{1,0:T(8,128)(2,1)S(1)}, u32[]{:S(2)}, u32[]{:S(2)}) collective-permute-start(bf16[96,2432]{1,0:T(8,128)(2,1)S(1)} %get-tuple-element.159), channel_id=1, source_target_pairs={{0,4},{1,5},{2,6},{3,7},{4,0},{5,1},{6,2},{7,3},{8,12},{9,13},{10,... | collective-permute-start | bytes 1400840 | tf_op jit(solution)/shard_map/ppermute | solution.py:26
  111.1 22.5 %collective-permute-start.37 = (bf16[96,2432]{1,0:T(8,128)(2,1)S(1)}, bf16[96,2432]{1,0:T(8,128)(2,1)S(1)}, u32[]{:S(2)}, u32[]{:S(2)}) collective-permute-start(bf16[96,2432]{1,0:T(8,128)(2,1)S(1)} %get-tuple-element.160), channel_id=1, source_target_pairs={{0,6},{1,7},{2,4},{3,5},{4,2},{5,3},{6,0},{7,1},{8,14},{9,15},{10,... | collective-permute-start | bytes 1400840 | tf_op jit(solution)/shard_map/ppermute | solution.py:26
  123.7 20.0 %collective-permute-start.40 = (bf16[96,768]{1,0:T(8,128)(2,1)S(1)}, bf16[96,768]{1,0:T(8,128)(2,1)S(1)}, u32[]{:S(2)}, u32[]{:S(2)}) collective-permute-start(bf16[96,768]{1,0:T(8,128)(2,1)S(1)} %get-tuple-element.173), channel_id=1, source_target_pairs={{0,2},{1,3},{2,0},{3,1},{4,6},{5,7},{6,4},{7,5},{8,10},{9,11},{10,... | collective-permute-start | bytes 442376 | tf_op jit(solution)/shard_map/ppermute | solution.py:26
  124.1 19.5 %collective-permute-start.41 = (bf16[96,768]{1,0:T(8,128)(2,1)S(1)}, bf16[96,768]{1,0:T(8,128)(2,1)S(1)}, u32[]{:S(2)}, u32[]{:S(2)}) collective-permute-start(bf16[96,768]{1,0:T(8,128)(2,1)S(1)} %get-tuple-element.174), channel_id=1, source_target_pairs={{0,4},{1,5},{2,6},{3,7},{4,0},{5,1},{6,2},{7,3},{8,12},{9,13},{10,... | collective-permute-start | bytes 442376 | tf_op jit(solution)/shard_map/ppermute | solution.py:26
  125.8 17.9 %collective-permute-start.42 = (bf16[96,768]{1,0:T(8,128)(2,1)S(1)}, bf16[96,768]{1,0:T(8,128)(2,1)S(1)}, u32[]{:S(2)}, u32[]{:S(2)}) collective-permute-start(bf16[96,768]{1,0:T(8,128)(2,1)S(1)} %get-tuple-element.175), channel_id=1, source_target_pairs={{0,6},{1,7},{2,4},{3,5},{4,2},{5,3},{6,0},{7,1},{8,14},{9,15},{10,... | collective-permute-start | bytes 442376 | tf_op jit(solution)/shard_map/ppermute | solution.py:26
  134.6 9.1 %collective-permute-start.43 = (bf16[48,2432]{1,0:T(8,128)(2,1)S(1)}, bf16[48,2432]{1,0:T(8,128)(2,1)S(1)}, u32[]{:S(2)}, u32[]{:S(2)}) collective-permute-start(bf16[48,2432]{1,0:T(8,128)(2,1)S(1)} %get-tuple-element.184), channel_id=1, source_target_pairs={{0,8},{8,0},{16,24},{24,16},{1,9},{9,1},{17,25},{25,17},{2,10},{10... | collective-permute-start | bytes 700424 | tf_op jit(solution)/shard_map/ppermute | solution.py:26
  143.9 12.0 %collective-permute-start.44 = (bf16[48,2432]{1,0:T(8,128)(2,1)S(1)}, bf16[48,2432]{1,0:T(8,128)(2,1)S(1)}, u32[]{:S(2)}, u32[]{:S(2)}) collective-permute-start(bf16[48,2432]{1,0:T(8,128)(2,1)S(1)} %total_sum.4.refs_0_), channel_id=1, source_target_pairs={{0,16},{8,24},{16,0},{24,8},{1,17},{9,25},{17,1},{25,9},{2,18},{10... | collective-permute-start | bytes 700424 | tf_op jit(solution)/shard_map/ppermute | solution.py:26
  146.8 6.7 %collective-permute-start.45 = (bf16[96,768]{1,0:T(8,128)(2,1)S(1)}, bf16[96,768]{1,0:T(8,128)(2,1)S(1)}, u32[]{:S(2)}, u32[]{:S(2)}) collective-permute-start(bf16[96,768]{1,0:T(8,128)(2,1)S(1)} %total_sum.5.refs_0_), channel_id=1, source_target_pairs={{0,8},{8,0},{16,24},{24,16},{1,9},{9,1},{17,25},{25,17},{2,10},{10... | collective-permute-start | bytes 442376 | tf_op jit(solution)/shard_map/ppermute | solution.py:26
  155.9 10.8 %collective-permute-start.47 = (bf16[48,2432]{1,0:T(8,128)(2,1)S(1)}, bf16[48,2432]{1,0:T(8,128)(2,1)S(1)}, u32[]{:S(2)}, u32[]{:S(2)}) collective-permute-start(bf16[48,2432]{1,0:T(8,128)(2,1)S(1)} %total_sum.7.tail_ref), channel_id=1, source_target_pairs={{0,8},{8,0},{16,24},{24,16},{1,9},{9,1},{17,25},{25,17},{2,10},{10... | collective-permute-start | bytes 700424 | tf_op jit(solution)/shard_map/ppermute | solution.py:26
  156.1 10.4 %collective-permute-start.46 = (bf16[96,768]{1,0:T(8,128)(2,1)S(1)}, bf16[96,768]{1,0:T(8,128)(2,1)S(1)}, u32[]{:S(2)}, u32[]{:S(2)}) collective-permute-start(bf16[96,768]{1,0:T(8,128)(2,1)S(1)} %total_sum.6.head_ref), channel_id=1, source_target_pairs={{0,24},{8,16},{16,8},{24,0},{1,25},{9,17},{17,9},{25,1},{2,26},{10... | collective-permute-start | bytes 442376 | tf_op jit(solution)/shard_map/ppermute | solution.py:26
  (34 other events, 154.2 us)
where the time goes:
time: 169 us
  Pallas kernels  77.4 us (46%)
  waiting for transfers between devices  46 us (27%)
  starting transfers between devices  38.5 us (23%)
  local copies, waits for them, and re-layouts  5.7 us (3%)
    pallas_call x19, Pallas kernels, call(): pl.pallas_call(body, in_specs=[SM if x.dtype == jnp.int32 else VM for x i...  70.7 us
    ppermute x48, waiting for transfers between devices, swap(): lax.ppermute(values, axis, [(place, place ^ bit) for place in range(size)])  46 us
    ppermute x48, starting transfers between devices, swap(): lax.ppermute(values, axis, [(place, place ^ bit) for place in range(size)])  38.5 us
    pallas_call x1, Pallas kernels, expert_grad(): pl.pallas_call(functools.partial(expert_grad_body, len(sources)), grid=(h...  6.66 us
    unnamed x20, local copies, waits for them, and re-layouts  3.94 us
  transfers between devices with their start and end apart: 48, of which 26 were waited for; matrix products, arithmetic and copies ran while one was open for 1% of the time, Pallas kernels for 25%

commit v1 on v0

--- a/solution.py
+++ b/solution.py
@@ -69,6 +69,10 @@
         - normed * jnp.mean(scaled * normed, axis=-1, keepdims=True)
     )
     return factor * inner
+
+
+def first_part(features):
+    return features // 3
 
 
 def pieces_of(rows, extra):
@@ -154,44 +158,53 @@
     )(*inputs)
 
 
-def prepare_body(in_ref, out_ref, router_ref, one_ref, two_ref, h0, h1, t0, t1):
+def prepare_body(in_hbm, out_hbm, small_ref, h0, h1, t0, t1, in_ref, out_ref, sems):
     rows, features = out_ref.shape
     half = rows // 2
-    part = features // 3
+    part = first_part(features)
+    rest = features - part
     extra = h0.shape[0] - half
-    small = [ref[...].astype(F32) for ref in (one_ref, two_ref, router_ref)]
-    small.append(jnp.zeros((extra - 2 - router_ref.shape[0], rows), F32))
-    small = jnp.concatenate(small, axis=0)
-    small = jnp.concatenate([small, jnp.zeros((extra, LANES - rows), F32)], axis=1)
     h0[:extra, :] = jnp.zeros((extra, h0.shape[1]), BF16)
-    h0[:extra, :LANES] = small.astype(BF16)
+    h0[:extra, :LANES] = small_ref[...]
+    copies = [
+        pltpu.make_async_copy(source, target, sems.at[k])
+        for k, (source, target) in enumerate(((in_hbm, in_ref), (out_hbm, out_ref)))
+    ]
+    for copy in copies:
+        copy.start()
+    for copy in copies:
+        copy.wait()
     for head, tail, start, here in ((h0, t0, extra, slice(0, half)), (h1, t1, 0, slice(half, rows))):
         for k in range(3):
             base = k * features
             head[start:, k * part : (k + 1) * part] = in_ref[here, base : base + part]
-            tail[:, 2 * k * part : 2 * (k + 1) * part] = in_ref[here, base + part : base + features]
-        tail[:, 2 * features :] = out_ref[here, :]
-
-
-def prepare(heads_in, heads_out, router, one, two):
+            tail[:, k * rest : (k + 1) * rest] = in_ref[here, base + part : base + features]
+        tail[:, 3 * rest :] = out_ref[here, :]
+
+
+def prepare(heads_in, heads_out, small):
     rows, features = heads_out.shape
-    extra = -(-(router.shape[0] + 2) // 16) * 16
-    inputs = (heads_in, heads_out, router, one, two)
+    part = first_part(features)
+    head, tail = 3 * part, 4 * features - 3 * part
     outputs = [
-        (extra + rows // 2, features),
-        (rows // 2, features),
-        (rows // 2, 3 * features),
-        (rows // 2, 3 * features),
+        (small.shape[0] + rows // 2, head),
+        (rows // 2, head),
+        (rows // 2, tail),
+        (rows // 2, tail),
     ]
     return pl.pallas_call(
         prepare_body,
-        grid=(1,),
-        in_specs=[pl.BlockSpec(x.shape, lambda i: (0, 0)) for x in inputs],
+        in_specs=[pl.BlockSpec(memory_space=pltpu.HBM)] * 2 + [VM],
         out_specs=[VM] * len(outputs),
         out_shape=[pltpu.VMEM(shape, BF16) for shape in outputs],
+        scratch_shapes=[
+            pltpu.VMEM(heads_in.shape, BF16),
+            pltpu.VMEM(heads_out.shape, BF16),
+            pltpu.SemaphoreType.DMA((2,)),
+        ],
         compiler_params=pltpu.CompilerParams(vmem_limit_bytes=4 * 1024 * 1024),
         name="prepare",
-    )(*inputs)
+    )(heads_in, heads_out, small)
 
 
 def join_body(a0, a1, b0, b1, a_ref, b_ref):
@@ -342,7 +355,7 @@
         packed_ref[group, :features] = dot(dispatch.astype(BF16), act).astype(BF16)
         packed_ref[group, features:] = dot(combine.astype(BF16), cot_ref[here, :]).astype(BF16)
 
-    each_image(images, 3, route_image)
+    each_image(images, 6, route_image)
 
     high = out_refs[0].shape[0]
     pick = pick_rows(
@@ -476,15 +489,16 @@
     odd = order_ref[order_ref.shape[0] - 2]
     tail[pl.ds(pl.multiple_of(odd * half, 16), half), :] = tail_ref[...].astype(F32)
     tail[pl.ds(pl.multiple_of((1 - odd) * half, 16), half), :] = tail_other[...].astype(F32)
-    part = features // 3
+    part = first_part(features)
+    left = features - part
     for k in range(3):
         here = slice(k * part, (k + 1) * part)
         in_ref[:, k * features : k * features + part] = (
             head_ref[:, here].astype(F32) + head_other[:, here].astype(F32)
         )
-        in_ref[:, k * features + part : (k + 1) * features] = tail[:, 2 * k * part : 2 * (k + 1) * part]
-    out_ref[...] = tail[:, 2 * features : 3 * features]
-    rest = tail[:, 3 * features :]
+        in_ref[:, k * features + part : (k + 1) * features] = tail[:, k * left : (k + 1) * left]
+    out_ref[...] = tail[:, 3 * left : 3 * left + features]
+    rest = tail[:, 3 * left + features :]
     rest = rest.T
     router_ref[...] = rest[:experts, :]
     gain_two_ref[...] = rest[experts : experts + 1, :]
@@ -494,7 +508,7 @@
 
 
 def shares(experts, order, head, head_other, tail, tail_other, w, gain):
-    rows, features = head.shape
+    rows, features = w.shape[0], w.shape[1] // 3
     return call(
         functools.partial(shares_body, experts),
         "shares",
@@ -761,7 +775,8 @@
         order = jnp.concatenate([ways, ways, odd[None], chip[None]])
     tall = -(-places // 16) * 16
     slot_rows = -(-experts // 16) * 16
-    part = features // 3
+    part = first_part(features)
+    rest = features - part
     wide = 3 * part
 
     grow = ((0, 0), (0, tall - places), (0, 0))
@@ -769,9 +784,10 @@
     cot = jnp.pad(cotangent, grow).reshape(images * tall, features)
     if direct:
         rows_in, order = lax.optimization_barrier((heads_in, order))
-        h0, h1, t0, t1 = prepare(
-            rows_in, heads_out, slot_router.T, first_gain[None], second_gain[None]
-        )
+        small = jnp.concatenate([first_gain[None], second_gain[None], slot_router.T], axis=0)
+        extra = -(-small.shape[0] // 16) * 16
+        small = jnp.pad(small, ((0, extra - small.shape[0]), (0, LANES - own_rows)))
+        h0, h1, t0, t1 = prepare(rows_in, heads_out, small)
         head_first = gather_first((h0, h1))
         head_first = after(head_first, source, cot)
         (t0, t1), head_first = lax.optimization_barrier(((t0, t1), head_first))
@@ -793,7 +809,7 @@
         small = jnp.pad(small, ((0, 0), (0, extra - small.shape[1]), (0, wide - small.shape[2])))
         head = as_gathered(jnp.concatenate([small, head_part], axis=1), extra + features // 16)
         tail_part = lax.all_gather(tail_part, "grp", axis=0, tiled=True)
-        tail = as_gathered(tail_part.reshape(8, -1, 3 * features), features // 16)
+        tail = as_gathered(tail_part.reshape(8, -1, 3 * rest + features), features // 16)
 
     act, small, w_head, joint_head, prob_head, mixed_head = attend(
         True, images, places, order, source, head, wide
@@ -802,7 +818,7 @@
         tail_second = after(gather_second(tail_join), mixed_head)
         tail = gather_last((t0, t1), tail_first, tail_second)
     w_out, w_tail, joint_tail, prob_tail, mixed_tail = attend(
-        False, images, places, order, act, tail, 2 * wide
+        False, images, places, order, act, tail, 3 * rest
     )
     mixes = [mixed_head, mixed_tail]
     resid, logits, *leaving = route(
@@ -815,7 +831,7 @@
     received, kept, given = expert(images, piece_in, piece_out, arrived)
     both = pair_sum(kept, [swap(given, "grp", group, 1)], experts)
     summed = [both[0]] + [swap(both[k], "grp", group, 2 * k) for k in range(1, experts)]
-    received = after(received, *summed)
+    received = after(received, *both)
     far = [swap(received, "rep", reps, k) for k in range(1, reps)]
     output, att, grad_mixed, grad_out, grad_side = back(
         images, places, experts, order, resid, logits, cot, mixes, w_out, small, summed
@@ -870,12 +886,13 @@
         columns = []
         for k in range(3):
             columns.append(head_sum[:, k * part : (k + 1) * part])
-            columns.append(tail_sum[:, 2 * k * part : 2 * (k + 1) * part])
+            columns.append(tail_sum[:, k * rest : (k + 1) * rest])
         heads_in_grad = jnp.concatenate(columns, axis=1)
         gain_one_grad = jnp.sum(heads_in_grad * heads_in.astype(F32), axis=1)
         gain_one_grad = gain_one_grad / first_gain.astype(F32)
-        heads_out_grad, rest = tail_sum[:, 2 * wide : 3 * wide], tail_sum[:, 3 * wide :]
-        router_grad, gain_two_grad = rest[:, :experts], rest[:, experts]
+        tail_sum = tail_sum[:, 3 * rest :]
+        heads_out_grad, tail_sum = tail_sum[:, :features], tail_sum[:, features:]
+        router_grad, gain_two_grad = tail_sum[:, :experts], tail_sum[:, experts]
     return (
         output,
         token_grad,

time: 169 us -> 163 us (0.964)
  waiting for transfers between devices: 46 us -> 42.4 us
  local copies, waits for them, and re-layouts: 5.7 us -> 3.7 us
    ppermute x48, waiting for transfers between devices: 46 us -> 42.4 us  [swap(): lax.ppermute(values, axis, [(place, place ^ bit) for place in range(size)])]
    unnamed x20 -> x14, local copies, waits for them, and re-layouts: 3.94 us -> 1.95 us
  transfers between devices with their start and end apart: 48 -> 48, of which waited for: 26 -> 22; matrix products, arithmetic and copies ran while one was open for 1% -> 1% of each run, Pallas kernels for 25% -> 26%
where the time goes in v1:
time: 163 us; the launch traced here: 162 us
  Pallas kernels  76.5 us (47%)
  waiting for transfers between devices  42.4 us (26%)
  starting transfers between devices  38.1 us (23%)
  local copies, waits for them, and re-layouts  3.7 us (2%)
    pallas_call x19, Pallas kernels, call(): pl.pallas_call(body, in_specs=[SM if x.dtype == jnp.int32 else VM for x i...  69.3 us
    ppermute x48, waiting for transfers between devices, swap(): lax.ppermute(values, axis, [(place, place ^ bit) for place in range(size)])  42.4 us
    ppermute x48, starting transfers between devices, swap(): lax.ppermute(values, axis, [(place, place ^ bit) for place in range(size)])  38.1 us
    pallas_call x1, Pallas kernels, expert_grad(): pl.pallas_call(functools.partial(expert_grad_body, len(sources)), grid=(h...  6.66 us
  transfers between devices with their start and end apart: 48, of which 22 were waited for; matrix products, arithmetic and copies ran while one was open for 1% of the time, Pallas kernels for 26%

profile of v1, /device:TPU:0, one launch (start us, length us, event | category | flops | bytes accessed | tf_op | source)
XLA Modules:
  0.0 162.5 jit_solution(5550873116609806410)
XLA Ops:
  3.9 3.0 %collective-permute-start = (bf16[64,768]{1,0:T(8,128)(2,1)S(1)}, bf16[64,768]{1,0:T(8,128)(2,1)S(1)}, u32[]{:S(2)}, u32[]{:S(2)}) collective-permute-start(bf16[64,768]{1,0:T(8,128)(2,1)S(1)} %get-tuple-element.111.a0.refs_0_), channel_id=1, source_target_pairs={{0,2},{1,3},{2,0},{3,1},{4,6},{5,7},{6,4},{7,5},{8,10},{9,11},{10,... | collective-permute-start | bytes 294920 | tf_op jit(solution)/shard_map/ppermute | solution.py:26
  8.4 1.6 %pad.11 = bf16[6,208,768]{2,1,0:T(8,128)(2,1)S(1)} pad(bf16[6,197,768]{2,1,0:T(8,128)(2,1)} %param.9, bf16[]{:T(256)} %constant.62.clone.1), padding=0_0x0_11x0_0 | pad | bytes 3732482 | tf_op jit(solution)/shard_map/jit(_pad)/pad | solution.py:783
  17.6 2.0 %collective-permute-done.5.refs_5_ = bf16[96,768]{1,0:T(8,128)(2,1)S(1)} collective-permute-done((bf16[96,768]{1,0:T(8,128)(2,1)S(1)}, bf16[96,768]{1,0:T(8,128)(2,1)S(1)}, u32[]{:S(2)}, u32[]{:S(2)}) %collective-permute-start.5) | collective-permute-done | bytes 147488 | tf_op jit(solution)/shard_map/ppermute | solution.py:26
  21.1 2.8 %collective-permute-done.2.a1.refs_2_ = bf16[48,2304]{1,0:T(8,128)(2,1)S(1)} collective-permute-done((bf16[48,2304]{1,0:T(8,128)(2,1)S(1)}, bf16[48,2304]{1,0:T(8,128)(2,1)S(1)}, u32[]{:S(2)}, u32[]{:S(2)}) %collective-permute-start.2) | collective-permute-done | bytes 221216 | tf_op jit(solution)/shard_map/ppermute | solution.py:26
  24.8 6.5 %attend.2 = (bf16[1248,768]{1,0:T(8,128)(2,1)S(1)}, f32[16,768]{1,0:T(8,128)S(1)}, bf16[768,768]{1,0:T(8,128)(2,1)S(1)}, bf16[1248,768]{1,0:T(8,128)(2,1)S(1)}, ...) custom-call(s32[18]{0:T(128)S(1)} %pad_add_fusion.order_ref, bf16[1248,768]{1,0:T(8,128)(2,1)S(1)} %bitcast.18, ...), custom_call_target="tpu_custom_call" | custom-call | flops 2944401408 | bytes 1000000 | tf_op jit(solution)/shard_map/attend/pallas_call | solution.py:146
  31.3 4.5 %collective-permute-done.12.refs_4_ = bf16[96,2304]{1,0:T(8,128)(2,1)S(1)} collective-permute-done((bf16[96,2304]{1,0:T(8,128)(2,1)S(1)}, bf16[96,2304]{1,0:T(8,128)(2,1)S(1)}, u32[]{:S(2)}, u32[]{:S(2)}) %collective-permute-start.12) | collective-permute-done | bytes 442400 | tf_op jit(solution)/shard_map/ppermute | solution.py:26
  37.1 1.7 %collective-permute-done.15.refs_7_ = bf16[48,2304]{1,0:T(8,128)(2,1)S(1)} collective-permute-done((bf16[48,2304]{1,0:T(8,128)(2,1)S(1)}, bf16[48,2304]{1,0:T(8,128)(2,1)S(1)}, u32[]{:S(2)}, u32[]{:S(2)}) %collective-permute-start.15) | collective-permute-done | bytes 221216 | tf_op jit(solution)/shard_map/ppermute | solution.py:26
  39.5 9.1 %attend.3 = (bf16[768,768]{1,0:T(8,128)(2,1)S(1)}, bf16[768,1536]{1,0:T(8,128)(2,1)S(1)}, bf16[1248,1536]{1,0:T(8,128)(2,1)S(1)}, bf16[48,208,208]{2,1,0:T(8,128)(2,1)S(1)}, bf16[1248,512]{1,0:T(8,128)(2,1)S(1)}) custom-call(s32[18]{0:T(128)S(1)} %pad_add_fusion.order_ref, bf16[1248,768]{1,0:T(8,128)(2,1)S(1)} %get-tuple-element.127.source_ref.act_ref, ...), custom_call_target="tpu_custom_call" | custom-call | flops 5888802816 | bytes 1000000 | tf_op jit(solution)/shard_map/attend/pallas_call | solution.py:146
  48.6 4.1 %route.1 = (f32[1248,768]{1,0:T(8,128)S(1)}, f32[96,208]{1,0:T(8,128)S(1)}, bf16[8,1536]{1,0:T(8,128)(2,1)S(1)}, bf16[8,1536]{1,0:T(8,128)(2,1)S(1)}, bf16[8,153...) custom-call(s32[18]{0:T(128)S(1)} %pad_add_fusion.order_ref, bf16[1248,768]{1,0:T(8,128)(2,1)S(1)} %bitcast.19, ...), custom_call_target="tpu_custom_call" | custom-call | flops 2944401408 | bytes 1000000 | tf_op jit(solution)/shard_map/route/pallas_call | solution.py:146
  53.1 1.7 %collective-permute-start.21 = (bf16[8,1536]{1,0:T(8,128)(2,1)S(1)}, bf16[8,1536]{1,0:T(8,128)(2,1)S(1)}, u32[]{:S(2)}, u32[]{:S(2)}) collective-permute-start(bf16[8,1536]{1,0:T(8,128)(2,1)S(1)} %get-tuple-element.137), channel_id=1, source_target_pairs={{0,4},{1,5},{2,6},{3,7},{4,0},{5,1},{6,2},{7,3},{8,12},{9,13},{10,... | collective-permute-start | bytes 73736 | tf_op jit(solution)/shard_map/ppermute | solution.py:26
  57.1 2.4 %collective-permute-done.22.refs_3_ = bf16[8,1536]{1,0:T(8,128)(2,1)S(1)} collective-permute-done((bf16[8,1536]{1,0:T(8,128)(2,1)S(1)}, bf16[8,1536]{1,0:T(8,128)(2,1)S(1)}, u32[]{:S(2)}, u32[]{:S(2)}) %collective-permute-start.22) | collective-permute-done | bytes 24608 | tf_op jit(solution)/shard_map/ppermute | solution.py:26
  60.7 2.4 %expert.1 = (bf16[48,1536]{1,0:T(8,128)(2,1)S(1)}, bf16[32,1536]{1,0:T(8,128)(2,1)S(1)}, bf16[32,1536]{1,0:T(8,128)(2,1)S(1)}) custom-call(bf16[768,1536]{1,0:T(8,128)(2,1)S(1)} %bitcast.14, bf16[1536,768]{1,0:T(8,128)(2,1)S(1)} %bitcast.16, bf16[8,1536]{1,0:T(8,128)(2,1)S(1)} %get-tuple-element.135.refs_0_, ...), custom_call_target="tpu_custom_call" | custom-call | flops 1000000000 | bytes 1000000 | tf_op jit(solution)/shard_map/expert/pallas_call | solution.py:146
  68.1 3.6 %collective-permute-start.33 = (bf16[48,1536]{1,0:T(8,128)(2,1)S(1)}, bf16[48,1536]{1,0:T(8,128)(2,1)S(1)}, u32[]{:S(2)}, u32[]{:S(2)}) collective-permute-start(bf16[48,1536]{1,0:T(8,128)(2,1)S(1)} %get-tuple-element.192.refs_0_), channel_id=1, source_target_pairs={{0,24},{8,16},{16,8},{24,0},{1,25},{9,17},{17,9},{25,1},{2,26},{10... | collective-permute-start | bytes 442376 | tf_op jit(solution)/shard_map/ppermute | solution.py:26
  72.5 10.9 %back.1 = (bf16[6,197,768]{2,1,0:T(8,128)(2,1)}, bf16[1248,768]{1,0:T(8,128)(2,1)S(1)}, bf16[1248,768]{1,0:T(8,128)(2,1)S(1)}, bf16[768,768]{1,0:T(8,128)(2,1)S(1)}, bf16[768,128]{1,0:T(8,128)(2,1)S(1)}) custom-call(s32[18]{0:T(128)S(1)} %pad_add_fusion.order_ref, f32[1248,768]{1,0:T(8,128)S(1)} %get-tuple-element.133.resid_ref, ...), custom_call_target="tpu_custom_call" | custom-call | flops 5888802816 | bytes 1000000 | tf_op jit(solution)/shard_map/back/pallas_call | solution.py:146
  83.7 16.2 %attend_back.2 = (bf16[1248,1536]{1,0:T(8,128)(2,1)S(1)}, bf16[384,2432]{1,0:T(8,128)(2,1)S(1)}, bf16[384,2432]{1,0:T(8,128)(2,1)S(1)}) custom-call(s32[18]{0:T(128)S(1)} %pad_add_fusion.order_ref, bf16[1248,1536]{1,0:T(8,128)(2,1)S(1)} %get-tuple-element.147.joint_ref, bf16[48,208,208]{2,1,0:T(8,128)(2,1)S(1)} %get-tuple-element.148.prob_ref, ...), custom_call_target="tpu_custom_call" | custom-call | flops 11777605632 | bytes 1000000 | tf_op jit(solution)/shard_map/attend_back/pallas_call | solution.py:146
  100.0 3.8 %collective-permute-done.34.refs_0_ = bf16[384,2432]{1,0:T(8,128)(2,1)S(1)} collective-permute-done((bf16[384,2432]{1,0:T(8,128)(2,1)S(1)}, bf16[384,2432]{1,0:T(8,128)(2,1)S(1)}, u32[]{:S(2)}, u32[]{:S(2)}) %collective-permute-start.34) | collective-permute-done | bytes 1867808 | tf_op jit(solution)/shard_map/ppermute | solution.py:26
  107.8 8.7 %attend_back.3 = (bf16[1248,768]{1,0:T(8,128)(2,1)S(1)}, bf16[384,768]{1,0:T(8,128)(2,1)S(1)}, bf16[192,768]{1,0:T(8,128)(2,1)S(1)}, bf16[192,768]{1,0:T(8,128)(2,1)S(1)}) custom-call(s32[18]{0:T(128)S(1)} %pad_add_fusion.order_ref, bf16[1248,768]{1,0:T(8,128)(2,1)S(1)} %get-tuple-element.161.joint_ref, ...), custom_call_target="tpu_custom_call" | custom-call | flops 5888802816 | bytes 1000000 | tf_op jit(solution)/shard_map/attend_back/pallas_call | solution.py:146
  122.3 7.2 %collective-permute-done.36.refs_2_ = bf16[96,2432]{1,0:T(8,128)(2,1)S(1)} collective-permute-done((bf16[96,2432]{1,0:T(8,128)(2,1)S(1)}, bf16[96,2432]{1,0:T(8,128)(2,1)S(1)}, u32[]{:S(2)}, u32[]{:S(2)}) %collective-permute-start.36) | collective-permute-done | bytes 466976 | tf_op jit(solution)/shard_map/ppermute | solution.py:26
  131.3 7.8 %finish.1 = bf16[6,197,768]{2,1,0:T(8,128)(2,1)} custom-call(bf16[1248,768]{1,0:T(8,128)(2,1)S(1)} %bitcast.20, bf16[1248,768]{1,0:T(8,128)(2,1)S(1)} %get-tuple-element.176.att_ref, bf16[1248,768]{1,0:T(8,128)(2,1)S(1)} %get-tuple-element.177.j0, bf16[1248,1536]{1,0:T(8,128)(2,1)S(1)} %get-tuple-element.178.j1, bf16[768,768]{1,0:T(8,128)(2,1)S(1)} %get-tuple-element.179.s0, ...), custom_call_target="tpu_custom_call" | custom-call | flops 4416602112 | bytes 1000000 | tf_op jit(solution)/shard_map/finish/pallas_call | solution.py:146
  139.3 3.2 %collective-permute-start.44 = (bf16[48,2432]{1,0:T(8,128)(2,1)S(1)}, bf16[48,2432]{1,0:T(8,128)(2,1)S(1)}, u32[]{:S(2)}, u32[]{:S(2)}) collective-permute-start(bf16[48,2432]{1,0:T(8,128)(2,1)S(1)} %total_sum.4.refs_0_), channel_id=1, source_target_pairs={{0,16},{8,24},{16,0},{24,8},{1,17},{9,25},{17,1},{25,9},{2,18},{10... | collective-permute-start | bytes 700424 | tf_op jit(solution)/shard_map/ppermute | solution.py:26
  142.7 6.7 %expert_grad.1 = (f32[768,1536]{1,0:T(8,128)}, f32[1536,768]{1,0:T(8,128)}) custom-call(bf16[48,1536]{1,0:T(8,128)(2,1)S(1)} %get-tuple-element.192.refs_0_, bf16[48,1536]{1,0:T(8,128)(2,1)S(1)} %collective-permute-done.31.refs_1_, bf16[48,1536]{1,0:T(8,128)(2,1)S(1)} %collective-permute-done.32.refs_2_, ...), custom_call_target="tpu_custom_call" | custom-call | flops 1887436800 | bytes 14000000 | tf_op jit(solution)/shard_map/expert_grad/pallas_call | solution.py:546
  151.3 1.8 %collective-permute-start.46 = (bf16[96,768]{1,0:T(8,128)(2,1)S(1)}, bf16[96,768]{1,0:T(8,128)(2,1)S(1)}, u32[]{:S(2)}, u32[]{:S(2)}) collective-permute-start(bf16[96,768]{1,0:T(8,128)(2,1)S(1)} %total_sum.6.head_ref), channel_id=1, source_target_pairs={{0,24},{8,16},{16,8},{24,0},{1,25},{9,17},{17,9},{25,1},{2,26},{10... | collective-permute-start | bytes 442376 | tf_op jit(solution)/shard_map/ppermute | solution.py:26
  153.1 7.6 %collective-permute-done.46.head_other = bf16[96,768]{1,0:T(8,128)(2,1)S(1)} collective-permute-done((bf16[96,768]{1,0:T(8,128)(2,1)S(1)}, bf16[96,768]{1,0:T(8,128)(2,1)S(1)}, u32[]{:S(2)}, u32[]{:S(2)}) %collective-permute-start.46) | collective-permute-done | bytes 147488 | tf_op jit(solution)/shard_map/ppermute | solution.py:26
  160.7 1.7 %shares.1 = (f32[96,2304]{1,0:T(8,128)}, f32[96,768]{1,0:T(8,128)}, f32[4,96]{1,0:T(4,128)}, f32[1,96]{1,0:T(1,128)}, f32[1,96]{1,0:T(1,128)}) custom-call(s32[18]{0:T(128)S(1)} %pad_add_fusion.order_ref, bf16[96,768]{1,0:T(8,128)(2,1)S(1)} %total_sum.6.head_ref, bf16[96,768]{1,0:T(8,128)(2,1)S(1)} %collective-permute-done.46.head_other, ...), custom_call_target="tpu_custom_call" | custom-call | flops 1000000 | bytes 1000000 | tf_op jit(solution)/shard_map/shares/pallas_call | solution.py:146
  (112 shorter events, 40.4 us)
Async XLA Ops:
  3.9 7.4 %collective-permute-start = (bf16[64,768]{1,0:T(8,128)(2,1)S(1)}, bf16[64,768]{1,0:T(8,128)(2,1)S(1)}, u32[]{:S(2)}, u32[]{:S(2)}) collective-permute-start(bf16[64,768]{1,0:T(8,128)(2,1)S(1)} %get-tuple-element.111.a0.refs_0_), channel_id=1, source_target_pairs={{0,2},{1,3},{2,0},{3,1},{4,6},{5,7},{6,4},{7,5},{8,10},{9,11},{10,... | collective-permute-start | bytes 294920 | tf_op jit(solution)/shard_map/ppermute | solution.py:26
  12.9 6.6 %collective-permute-start.5 = (bf16[96,768]{1,0:T(8,128)(2,1)S(1)}, bf16[96,768]{1,0:T(8,128)(2,1)S(1)}, u32[]{:S(2)}, u32[]{:S(2)}) collective-permute-start(bf16[96,768]{1,0:T(8,128)(2,1)S(1)} %get-tuple-element.120), channel_id=1, source_target_pairs={{0,2},{1,3},{2,0},{3,1},{4,6},{5,7},{6,4},{7,5},{8,10},{9,11},{10,... | collective-permute-start | bytes 442376 | tf_op jit(solution)/shard_map/ppermute | solution.py:26
  13.7 10.2 %collective-permute-start.2 = (bf16[48,2304]{1,0:T(8,128)(2,1)S(1)}, bf16[48,2304]{1,0:T(8,128)(2,1)S(1)}, u32[]{:S(2)}, u32[]{:S(2)}) collective-permute-start(bf16[48,2304]{1,0:T(8,128)(2,1)S(1)} %get-tuple-element.115.a0.refs_0_), channel_id=1, source_target_pairs={{0,2},{1,3},{2,0},{3,1},{4,6},{5,7},{6,4},{7,5},{8,10},{9,11},{10,... | collective-permute-start | bytes 663560 | tf_op jit(solution)/shard_map/ppermute | solution.py:26
  15.2 8.7 %collective-permute-start.3 = (bf16[48,2304]{1,0:T(8,128)(2,1)S(1)}, bf16[48,2304]{1,0:T(8,128)(2,1)S(1)}, u32[]{:S(2)}, u32[]{:S(2)}) collective-permute-start(bf16[48,2304]{1,0:T(8,128)(2,1)S(1)} %get-tuple-element.116.b0.refs_1_), channel_id=1, source_target_pairs={{0,4},{1,5},{2,6},{3,7},{4,0},{5,1},{6,2},{7,3},{8,12},{9,13},{10,... | collective-permute-start | bytes 663560 | tf_op jit(solution)/shard_map/ppermute | solution.py:26
  17.0 6.9 %collective-permute-start.10 = (bf16[128,768]{1,0:T(8,128)(2,1)S(1)}, bf16[128,768]{1,0:T(8,128)(2,1)S(1)}, u32[]{:S(2)}, u32[]{:S(2)}) collective-permute-start(bf16[128,768]{1,0:T(8,128)(2,1)S(1)} %collective-permute-done.4.refs_4_), channel_id=1, source_target_pairs={{0,1},{1,0},{2,3},{3,2},{4,5},{5,4},{6,7},{7,6},{8,9},{9,8},{10,11... | collective-permute-start | bytes 589832 | tf_op jit(solution)/shard_map/ppermute | solution.py:26
  24.0 11.9 %collective-permute-start.12 = (bf16[96,2304]{1,0:T(8,128)(2,1)S(1)}, bf16[96,2304]{1,0:T(8,128)(2,1)S(1)}, u32[]{:S(2)}, u32[]{:S(2)}) collective-permute-start(bf16[96,2304]{1,0:T(8,128)(2,1)S(1)} %get-tuple-element.123), channel_id=1, source_target_pairs={{0,4},{1,5},{2,6},{3,7},{4,0},{5,1},{6,2},{7,3},{8,12},{9,13},{10,... | collective-permute-start | bytes 1327112 | tf_op jit(solution)/shard_map/ppermute | solution.py:26
  24.6 11.5 %collective-permute-start.13 = (bf16[96,2304]{1,0:T(8,128)(2,1)S(1)}, bf16[96,2304]{1,0:T(8,128)(2,1)S(1)}, u32[]{:S(2)}, u32[]{:S(2)}) collective-permute-start(bf16[96,2304]{1,0:T(8,128)(2,1)S(1)} %get-tuple-element.124), channel_id=1, source_target_pairs={{0,2},{1,3},{2,0},{3,1},{4,6},{5,7},{6,4},{7,5},{8,10},{9,11},{10,... | collective-permute-start | bytes 1327112 | tf_op jit(solution)/shard_map/ppermute | solution.py:26
  24.8 12.3 %collective-permute-start.14 = (bf16[48,2304]{1,0:T(8,128)(2,1)S(1)}, bf16[48,2304]{1,0:T(8,128)(2,1)S(1)}, u32[]{:S(2)}, u32[]{:S(2)}) collective-permute-start(bf16[48,2304]{1,0:T(8,128)(2,1)S(1)} %get-tuple-element.115.a0.refs_0_), channel_id=1, source_target_pairs={{0,1},{1,0},{2,3},{3,2},{4,5},{5,4},{6,7},{7,6},{8,9},{9,8},{10,11... | collective-permute-start | bytes 663560 | tf_op jit(solution)/shard_map/ppermute | solution.py:26
  64.6 7.2 %collective-permute-start.28 = (bf16[8,1536]{1,0:T(8,128)(2,1)S(1)}, bf16[8,1536]{1,0:T(8,128)(2,1)S(1)}, u32[]{:S(2)}, u32[]{:S(2)}) collective-permute-start(bf16[8,1536]{1,0:T(8,128)(2,1)S(1)} %get-tuple-element.142), channel_id=1, source_target_pairs={{0,2},{1,3},{2,0},{3,1},{4,6},{5,7},{6,4},{7,5},{8,10},{9,11},{10,... | collective-permute-start | bytes 73736 | tf_op jit(solution)/shard_map/ppermute | solution.py:26
  66.1 6.4 %collective-permute-start.29 = (bf16[8,1536]{1,0:T(8,128)(2,1)S(1)}, bf16[8,1536]{1,0:T(8,128)(2,1)S(1)}, u32[]{:S(2)}, u32[]{:S(2)}) collective-permute-start(bf16[8,1536]{1,0:T(8,128)(2,1)S(1)} %get-tuple-element.143), channel_id=1, source_target_pairs={{0,4},{1,5},{2,6},{3,7},{4,0},{5,1},{6,2},{7,3},{8,12},{9,13},{10,... | collective-permute-start | bytes 73736 | tf_op jit(solution)/shard_map/ppermute | solution.py:26
  68.1 15.3 %collective-permute-start.33 = (bf16[48,1536]{1,0:T(8,128)(2,1)S(1)}, bf16[48,1536]{1,0:T(8,128)(2,1)S(1)}, u32[]{:S(2)}, u32[]{:S(2)}) collective-permute-start(bf16[48,1536]{1,0:T(8,128)(2,1)S(1)} %get-tuple-element.192.refs_0_), channel_id=1, source_target_pairs={{0,24},{8,16},{16,8},{24,0},{1,25},{9,17},{17,9},{25,1},{2,26},{10... | collective-permute-start | bytes 442376 | tf_op jit(solution)/shard_map/ppermute | solution.py:26
  71.7 12.0 %collective-permute-start.32 = (bf16[48,1536]{1,0:T(8,128)(2,1)S(1)}, bf16[48,1536]{1,0:T(8,128)(2,1)S(1)}, u32[]{:S(2)}, u32[]{:S(2)}) collective-permute-start(bf16[48,1536]{1,0:T(8,128)(2,1)S(1)} %get-tuple-element.192.refs_0_), channel_id=1, source_target_pairs={{0,16},{8,24},{16,0},{24,8},{1,17},{9,25},{17,1},{25,9},{2,18},{10... | collective-permute-start | bytes 442376 | tf_op jit(solution)/shard_map/ppermute | solution.py:26
  71.7 12.0 %collective-permute-start.31 = (bf16[48,1536]{1,0:T(8,128)(2,1)S(1)}, bf16[48,1536]{1,0:T(8,128)(2,1)S(1)}, u32[]{:S(2)}, u32[]{:S(2)}) collective-permute-start(bf16[48,1536]{1,0:T(8,128)(2,1)S(1)} %get-tuple-element.192.refs_0_), channel_id=1, source_target_pairs={{0,8},{8,0},{16,24},{24,16},{1,9},{9,1},{17,25},{25,17},{2,10},{10... | collective-permute-start | bytes 442376 | tf_op jit(solution)/shard_map/ppermute | solution.py:26
  104.3 16.5 %collective-permute-start.35 = (bf16[96,2432]{1,0:T(8,128)(2,1)S(1)}, bf16[96,2432]{1,0:T(8,128)(2,1)S(1)}, u32[]{:S(2)}, u32[]{:S(2)}) collective-permute-start(bf16[96,2432]{1,0:T(8,128)(2,1)S(1)} %get-tuple-element.158), channel_id=1, source_target_pairs={{0,2},{1,3},{2,0},{3,1},{4,6},{5,7},{6,4},{7,5},{8,10},{9,11},{10,... | collective-permute-start | bytes 1400840 | tf_op jit(solution)/shard_map/ppermute | solution.py:26
  105.8 23.6 %collective-permute-start.36 = (bf16[96,2432]{1,0:T(8,128)(2,1)S(1)}, bf16[96,2432]{1,0:T(8,128)(2,1)S(1)}, u32[]{:S(2)}, u32[]{:S(2)}) collective-permute-start(bf16[96,2432]{1,0:T(8,128)(2,1)S(1)} %get-tuple-element.159), channel_id=1, source_target_pairs={{0,4},{1,5},{2,6},{3,7},{4,0},{5,1},{6,2},{7,3},{8,12},{9,13},{10,... | collective-permute-start | bytes 1400840 | tf_op jit(solution)/shard_map/ppermute | solution.py:26
  106.3 23.1 %collective-permute-start.37 = (bf16[96,2432]{1,0:T(8,128)(2,1)S(1)}, bf16[96,2432]{1,0:T(8,128)(2,1)S(1)}, u32[]{:S(2)}, u32[]{:S(2)}) collective-permute-start(bf16[96,2432]{1,0:T(8,128)(2,1)S(1)} %get-tuple-element.160), channel_id=1, source_target_pairs={{0,6},{1,7},{2,4},{3,5},{4,2},{5,3},{6,0},{7,1},{8,14},{9,15},{10,... | collective-permute-start | bytes 1400840 | tf_op jit(solution)/shard_map/ppermute | solution.py:26
  118.7 20.4 %collective-permute-start.40 = (bf16[96,768]{1,0:T(8,128)(2,1)S(1)}, bf16[96,768]{1,0:T(8,128)(2,1)S(1)}, u32[]{:S(2)}, u32[]{:S(2)}) collective-permute-start(bf16[96,768]{1,0:T(8,128)(2,1)S(1)} %get-tuple-element.173), channel_id=1, source_target_pairs={{0,2},{1,3},{2,0},{3,1},{4,6},{5,7},{6,4},{7,5},{8,10},{9,11},{10,... | collective-permute-start | bytes 442376 | tf_op jit(solution)/shard_map/ppermute | solution.py:26
  120.3 18.8 %collective-permute-start.41 = (bf16[96,768]{1,0:T(8,128)(2,1)S(1)}, bf16[96,768]{1,0:T(8,128)(2,1)S(1)}, u32[]{:S(2)}, u32[]{:S(2)}) collective-permute-start(bf16[96,768]{1,0:T(8,128)(2,1)S(1)} %get-tuple-element.174), channel_id=1, source_target_pairs={{0,4},{1,5},{2,6},{3,7},{4,0},{5,1},{6,2},{7,3},{8,12},{9,13},{10,... | collective-permute-start | bytes 442376 | tf_op jit(solution)/shard_map/ppermute | solution.py:26
  120.8 18.3 %collective-permute-start.42 = (bf16[96,768]{1,0:T(8,128)(2,1)S(1)}, bf16[96,768]{1,0:T(8,128)(2,1)S(1)}, u32[]{:S(2)}, u32[]{:S(2)}) collective-permute-start(bf16[96,768]{1,0:T(8,128)(2,1)S(1)} %get-tuple-element.175), channel_id=1, source_target_pairs={{0,6},{1,7},{2,4},{3,5},{4,2},{5,3},{6,0},{7,1},{8,14},{9,15},{10,... | collective-permute-start | bytes 442376 | tf_op jit(solution)/shard_map/ppermute | solution.py:26
  130.4 8.7 %collective-permute-start.43 = (bf16[48,2432]{1,0:T(8,128)(2,1)S(1)}, bf16[48,2432]{1,0:T(8,128)(2,1)S(1)}, u32[]{:S(2)}, u32[]{:S(2)}) collective-permute-start(bf16[48,2432]{1,0:T(8,128)(2,1)S(1)} %get-tuple-element.184), channel_id=1, source_target_pairs={{0,8},{8,0},{16,24},{24,16},{1,9},{9,1},{17,25},{25,17},{2,10},{10... | collective-permute-start | bytes 700424 | tf_op jit(solution)/shard_map/ppermute | solution.py:26
  139.3 11.5 %collective-permute-start.44 = (bf16[48,2432]{1,0:T(8,128)(2,1)S(1)}, bf16[48,2432]{1,0:T(8,128)(2,1)S(1)}, u32[]{:S(2)}, u32[]{:S(2)}) collective-permute-start(bf16[48,2432]{1,0:T(8,128)(2,1)S(1)} %total_sum.4.refs_0_), channel_id=1, source_target_pairs={{0,16},{8,24},{16,0},{24,8},{1,17},{9,25},{17,1},{25,9},{2,18},{10... | collective-permute-start | bytes 700424 | tf_op jit(solution)/shard_map/ppermute | solution.py:26
  142.5 8.3 %collective-permute-start.45 = (bf16[96,768]{1,0:T(8,128)(2,1)S(1)}, bf16[96,768]{1,0:T(8,128)(2,1)S(1)}, u32[]{:S(2)}, u32[]{:S(2)}) collective-permute-start(bf16[96,768]{1,0:T(8,128)(2,1)S(1)} %total_sum.5.refs_0_), channel_id=1, source_target_pairs={{0,8},{8,0},{16,24},{24,16},{1,9},{9,1},{17,25},{25,17},{2,10},{10... | collective-permute-start | bytes 442376 | tf_op jit(solution)/shard_map/ppermute | solution.py:26
  150.8 9.9 %collective-permute-start.47 = (bf16[48,2432]{1,0:T(8,128)(2,1)S(1)}, bf16[48,2432]{1,0:T(8,128)(2,1)S(1)}, u32[]{:S(2)}, u32[]{:S(2)}) collective-permute-start(bf16[48,2432]{1,0:T(8,128)(2,1)S(1)} %total_sum.7.tail_ref), channel_id=1, source_target_pairs={{0,8},{8,0},{16,24},{24,16},{1,9},{9,1},{17,25},{25,17},{2,10},{10... | collective-permute-start | bytes 700424 | tf_op jit(solution)/shard_map/ppermute | solution.py:26
  151.3 9.4 %collective-permute-start.46 = (bf16[96,768]{1,0:T(8,128)(2,1)S(1)}, bf16[96,768]{1,0:T(8,128)(2,1)S(1)}, u32[]{:S(2)}, u32[]{:S(2)}) collective-permute-start(bf16[96,768]{1,0:T(8,128)(2,1)S(1)} %total_sum.6.head_ref), channel_id=1, source_target_pairs={{0,24},{8,16},{16,8},{24,0},{1,25},{9,17},{17,9},{25,1},{2,26},{10... | collective-permute-start | bytes 442376 | tf_op jit(solution)/shard_map/ppermute | solution.py:26
  (31 other events, 150.8 us)

commit v2 on v1

--- a/solution.py
+++ b/solution.py
@@ -152,7 +152,7 @@
             for n, (shape, kind) in enumerate(outputs)
         ],
         scratch_shapes=[pltpu.VMEM(shape, kind) for shape, kind in scratch],
-        compiler_params=pltpu.CompilerParams(vmem_limit_bytes=min(limit, 10) * 1024 * 1024),
+        compiler_params=pltpu.CompilerParams(vmem_limit_bytes=(limit if limit == 13 else min(limit, 10)) * 1024 * 1024),
         cost_estimate=pl.CostEstimate(flops=int(flops), bytes_accessed=1000000, transcendentals=0),
         name=name,
     )(*inputs)
@@ -300,7 +300,7 @@
         outputs,
         [],
         12,
-        2 * total * features * width * 2,
+        1 if first else 2 * total * features * width * 2,
     )
 
 
@@ -609,7 +609,7 @@
             gain_sum + jnp.sum(grad_act * normed, axis=0, keepdims=True),
         )
 
-    together = 3 if images % 3 == 0 else 1
+    together = 6 if images % 6 == 0 else 1
 
     def some(step, carry):
         for k in range(together):
@@ -648,7 +648,7 @@
             ((features, LANES), BF16),
         ],
         [((logits.shape[0], 2 * features), BF16)],
-        14,
+        13,
         8 * total * features * features,
         hbm=(0,),
     )
@@ -790,11 +790,10 @@
         h0, h1, t0, t1 = prepare(rows_in, heads_out, small)
         head_first = gather_first((h0, h1))
         head_first = after(head_first, source, cot)
-        (t0, t1), head_first = lax.optimization_barrier(((t0, t1), head_first))
         head_second = gather_second(join((h0, h1), head_first))
         tail_first = gather_first((t0, t1))
+        head_second, tail_first = lax.optimization_barrier((head_second, tail_first))
         head = gather_last((h0, h1), head_first, head_second)
-        tail_first = after(tail_first, *head)
         tail_join = join((t0, t1), tail_first)
         source = after(source, *tail_join)
     else:

time: 163 us -> 159 us (0.975)
  waiting for transfers between devices: 42.4 us -> 40.5 us
    ppermute x48, waiting for transfers between devices: 42.4 us -> 40.5 us  [swap(): lax.ppermute(values, axis, [(place, place ^ bit) for place in range(size)])]
  transfers between devices with their start and end apart: 48 -> 48, of which waited for: 22 -> 24; matrix products, arithmetic and copies ran while one was open for 1% -> 1% of each run, Pallas kernels for 26% -> 25%
where the time goes in v2:
time: 159 us
  Pallas kernels  74.9 us (47%)
  waiting for transfers between devices  40.5 us (25%)
  starting transfers between devices  37.8 us (24%)
  local copies, waits for them, and re-layouts  3.7 us (2%)
    pallas_call x19, Pallas kernels, call(): pl.pallas_call(body, in_specs=[SM if x.dtype == jnp.int32 else VM for x i...  67.7 us
    ppermute x48, waiting for transfers between devices, swap(): lax.ppermute(values, axis, [(place, place ^ bit) for place in range(size)])  40.5 us
    ppermute x48, starting transfers between devices, swap(): lax.ppermute(values, axis, [(place, place ^ bit) for place in range(size)])  37.8 us
    pallas_call x1, Pallas kernels, expert_grad(): pl.pallas_call(functools.partial(expert_grad_body, len(sources)), grid=(h...  6.66 us
  transfers between devices with their start and end apart: 48, of which 24 were waited for; matrix products, arithmetic and copies ran while one was open for 1% of the time, Pallas kernels for 25%

profile of v2, /device:TPU:0, one launch (start us, length us, event | category | flops | bytes accessed | tf_op | source)
XLA Modules:
  0.0 158.7 jit_solution(11598929299736207754)
XLA Ops:
  3.9 3.0 %collective-permute-start = (bf16[64,768]{1,0:T(8,128)(2,1)S(1)}, bf16[64,768]{1,0:T(8,128)(2,1)S(1)}, u32[]{:S(2)}, u32[]{:S(2)}) collective-permute-start(bf16[64,768]{1,0:T(8,128)(2,1)S(1)} %get-tuple-element.108.a0.refs_0_), channel_id=1, source_target_pairs={{0,2},{1,3},{2,0},{3,1},{4,6},{5,7},{6,4},{7,5},{8,10},{9,11},{10,... | collective-permute-start | bytes 294920 | tf_op jit(solution)/shard_map/ppermute | solution.py:26
  9.0 1.6 %pad.11 = bf16[6,208,768]{2,1,0:T(8,128)(2,1)S(1)} pad(bf16[6,197,768]{2,1,0:T(8,128)(2,1)} %param.9, bf16[]{:T(256)} %constant.62.clone.1), padding=0_0x0_11x0_0 | pad | bytes 3732482 | tf_op jit(solution)/shard_map/jit(_pad)/pad | solution.py:783
  12.0 1.7 %collective-permute-start.2 = (bf16[128,768]{1,0:T(8,128)(2,1)S(1)}, bf16[128,768]{1,0:T(8,128)(2,1)S(1)}, u32[]{:S(2)}, u32[]{:S(2)}) collective-permute-start(bf16[128,768]{1,0:T(8,128)(2,1)S(1)} %get-tuple-element.112), channel_id=1, source_target_pairs={{0,4},{1,5},{2,6},{3,7},{4,0},{5,1},{6,2},{7,3},{8,12},{9,13},{10,... | collective-permute-start | bytes 589832 | tf_op jit(solution)/shard_map/ppermute | solution.py:26
  14.4 1.7 %collective-permute-done.4.a1.refs_2_ = bf16[48,2304]{1,0:T(8,128)(2,1)S(1)} collective-permute-done((bf16[48,2304]{1,0:T(8,128)(2,1)S(1)}, bf16[48,2304]{1,0:T(8,128)(2,1)S(1)}, u32[]{:S(2)}, u32[]{:S(2)}) %collective-permute-start.4) | collective-permute-done | bytes 221216 | tf_op jit(solution)/shard_map/ppermute | solution.py:26
  17.3 1.5 collective-permute-done.3.refs_5_
  26.4 6.5 %attend.2 = (bf16[1248,768]{1,0:T(8,128)(2,1)S(1)}, f32[16,768]{1,0:T(8,128)S(1)}, bf16[768,768]{1,0:T(8,128)(2,1)S(1)}, bf16[1248,768]{1,0:T(8,128)(2,1)S(1)}, ...) custom-call(s32[18]{0:T(128)S(1)} %pad_add_fusion.order_ref, bf16[1248,768]{1,0:T(8,128)(2,1)S(1)} %bitcast.14, ...), custom_call_target="tpu_custom_call" | custom-call | flops 1 | bytes 1000000 | tf_op jit(solution)/shard_map/attend/pallas_call | solution.py:146
  36.3 9.1 %attend.3 = (bf16[768,768]{1,0:T(8,128)(2,1)S(1)}, bf16[768,1536]{1,0:T(8,128)(2,1)S(1)}, bf16[1248,1536]{1,0:T(8,128)(2,1)S(1)}, bf16[48,208,208]{2,1,0:T(8,128)(2,1)S(1)}, bf16[1248,512]{1,0:T(8,128)(2,1)S(1)}) custom-call(s32[18]{0:T(128)S(1)} %pad_add_fusion.order_ref, bf16[1248,768]{1,0:T(8,128)(2,1)S(1)} %get-tuple-element.123.source_ref.act_ref, ...), custom_call_target="tpu_custom_call" | custom-call | flops 5888802816 | bytes 1000000 | tf_op jit(solution)/shard_map/attend/pallas_call | solution.py:146
  45.5 4.1 %route.1 = (f32[1248,768]{1,0:T(8,128)S(1)}, f32[96,208]{1,0:T(8,128)S(1)}, bf16[8,1536]{1,0:T(8,128)(2,1)S(1)}, bf16[8,1536]{1,0:T(8,128)(2,1)S(1)}, bf16[8,153...) custom-call(s32[18]{0:T(128)S(1)} %pad_add_fusion.order_ref, bf16[1248,768]{1,0:T(8,128)(2,1)S(1)} %bitcast.15, ...), custom_call_target="tpu_custom_call" | custom-call | flops 2944401408 | bytes 1000000 | tf_op jit(solution)/shard_map/route/pallas_call | solution.py:146
  54.3 2.0 %collective-permute-done.22.refs_3_ = bf16[8,1536]{1,0:T(8,128)(2,1)S(1)} collective-permute-done((bf16[8,1536]{1,0:T(8,128)(2,1)S(1)}, bf16[8,1536]{1,0:T(8,128)(2,1)S(1)}, u32[]{:S(2)}, u32[]{:S(2)}) %collective-permute-start.22) | collective-permute-done | bytes 24608 | tf_op jit(solution)/shard_map/ppermute | solution.py:26
  57.6 2.4 %expert.1 = (bf16[48,1536]{1,0:T(8,128)(2,1)S(1)}, bf16[32,1536]{1,0:T(8,128)(2,1)S(1)}, bf16[32,1536]{1,0:T(8,128)(2,1)S(1)}) custom-call(bf16[768,1536]{1,0:T(8,128)(2,1)S(1)} %bitcast.17, bf16[1536,768]{1,0:T(8,128)(2,1)S(1)} %bitcast.19, bf16[8,1536]{1,0:T(8,128)(2,1)S(1)} %get-tuple-element.131.refs_0_, ...), custom_call_target="tpu_custom_call" | custom-call | flops 1000000000 | bytes 1000000 | tf_op jit(solution)/shard_map/expert/pallas_call | solution.py:146
  65.0 3.6 %collective-permute-start.33 = (bf16[48,1536]{1,0:T(8,128)(2,1)S(1)}, bf16[48,1536]{1,0:T(8,128)(2,1)S(1)}, u32[]{:S(2)}, u32[]{:S(2)}) collective-permute-start(bf16[48,1536]{1,0:T(8,128)(2,1)S(1)} %get-tuple-element.188.refs_0_), channel_id=1, source_target_pairs={{0,24},{8,16},{16,8},{24,0},{1,25},{9,17},{17,9},{25,1},{2,26},{10... | collective-permute-start | bytes 442376 | tf_op jit(solution)/shard_map/ppermute | solution.py:26
  69.4 9.3 %back.1 = (bf16[6,197,768]{2,1,0:T(8,128)(2,1)}, bf16[1248,768]{1,0:T(8,128)(2,1)S(1)}, bf16[1248,768]{1,0:T(8,128)(2,1)S(1)}, bf16[768,768]{1,0:T(8,128)(2,1)S(1)}, bf16[768,128]{1,0:T(8,128)(2,1)S(1)}) custom-call(s32[18]{0:T(128)S(1)} %pad_add_fusion.order_ref, f32[1248,768]{1,0:T(8,128)S(1)} %get-tuple-element.129.resid_ref, ...), custom_call_target="tpu_custom_call" | custom-call | flops 5888802816 | bytes 1000000 | tf_op jit(solution)/shard_map/back/pallas_call | solution.py:146
  78.7 1.9 %collective-permute-done.32.refs_2_ = bf16[48,1536]{1,0:T(8,128)(2,1)S(1)} collective-permute-done((bf16[48,1536]{1,0:T(8,128)(2,1)S(1)}, bf16[48,1536]{1,0:T(8,128)(2,1)S(1)}, u32[]{:S(2)}, u32[]{:S(2)}) %collective-permute-start.32) | collective-permute-done | bytes 147488 | tf_op jit(solution)/shard_map/ppermute | solution.py:26
  80.5 16.0 %attend_back.2 = (bf16[1248,1536]{1,0:T(8,128)(2,1)S(1)}, bf16[384,2432]{1,0:T(8,128)(2,1)S(1)}, bf16[384,2432]{1,0:T(8,128)(2,1)S(1)}) custom-call(s32[18]{0:T(128)S(1)} %pad_add_fusion.order_ref, bf16[1248,1536]{1,0:T(8,128)(2,1)S(1)} %get-tuple-element.143.joint_ref, bf16[48,208,208]{2,1,0:T(8,128)(2,1)S(1)} %get-tuple-element.144.prob_ref, ...), custom_call_target="tpu_custom_call" | custom-call | flops 11777605632 | bytes 1000000 | tf_op jit(solution)/shard_map/attend_back/pallas_call | solution.py:146
  96.6 3.8 %collective-permute-done.34.refs_0_ = bf16[384,2432]{1,0:T(8,128)(2,1)S(1)} collective-permute-done((bf16[384,2432]{1,0:T(8,128)(2,1)S(1)}, bf16[384,2432]{1,0:T(8,128)(2,1)S(1)}, u32[]{:S(2)}, u32[]{:S(2)}) %collective-permute-start.34) | collective-permute-done | bytes 1867808 | tf_op jit(solution)/shard_map/ppermute | solution.py:26
  104.4 8.6 %attend_back.3 = (bf16[1248,768]{1,0:T(8,128)(2,1)S(1)}, bf16[384,768]{1,0:T(8,128)(2,1)S(1)}, bf16[192,768]{1,0:T(8,128)(2,1)S(1)}, bf16[192,768]{1,0:T(8,128)(2,1)S(1)}) custom-call(s32[18]{0:T(128)S(1)} %pad_add_fusion.order_ref, bf16[1248,768]{1,0:T(8,128)(2,1)S(1)} %get-tuple-element.157.joint_ref, ...), custom_call_target="tpu_custom_call" | custom-call | flops 5888802816 | bytes 1000000 | tf_op jit(solution)/shard_map/attend_back/pallas_call | solution.py:146
  118.9 4.7 %collective-permute-done.36.refs_2_ = bf16[96,2432]{1,0:T(8,128)(2,1)S(1)} collective-permute-done((bf16[96,2432]{1,0:T(8,128)(2,1)S(1)}, bf16[96,2432]{1,0:T(8,128)(2,1)S(1)}, u32[]{:S(2)}, u32[]{:S(2)}) %collective-permute-start.36) | collective-permute-done | bytes 466976 | tf_op jit(solution)/shard_map/ppermute | solution.py:26
  125.9 8.1 %finish.1 = bf16[6,197,768]{2,1,0:T(8,128)(2,1)} custom-call(bf16[1248,768]{1,0:T(8,128)(2,1)S(1)} %bitcast.16, bf16[1248,768]{1,0:T(8,128)(2,1)S(1)} %get-tuple-element.172.att_ref, bf16[1248,768]{1,0:T(8,128)(2,1)S(1)} %get-tuple-element.173.j0, bf16[1248,1536]{1,0:T(8,128)(2,1)S(1)} %get-tuple-element.174.j1, bf16[768,768]{1,0:T(8,128)(2,1)S(1)} %get-tuple-element.175.s0, ...), custom_call_target="tpu_custom_call" | custom-call | flops 4416602112 | bytes 1000000 | tf_op jit(solution)/shard_map/finish/pallas_call | solution.py:146
  134.2 2.8 %collective-permute-start.44 = (bf16[48,2432]{1,0:T(8,128)(2,1)S(1)}, bf16[48,2432]{1,0:T(8,128)(2,1)S(1)}, u32[]{:S(2)}, u32[]{:S(2)}) collective-permute-start(bf16[48,2432]{1,0:T(8,128)(2,1)S(1)} %total_sum.4.refs_0_), channel_id=1, source_target_pairs={{0,16},{8,24},{16,0},{24,8},{1,17},{9,25},{17,1},{25,9},{2,18},{10... | collective-permute-start | bytes 700424 | tf_op jit(solution)/shard_map/ppermute | solution.py:26
  137.3 6.7 %expert_grad.1 = (f32[768,1536]{1,0:T(8,128)}, f32[1536,768]{1,0:T(8,128)}) custom-call(bf16[48,1536]{1,0:T(8,128)(2,1)S(1)} %get-tuple-element.188.refs_0_, bf16[48,1536]{1,0:T(8,128)(2,1)S(1)} %collective-permute-done.31.refs_1_, bf16[48,1536]{1,0:T(8,128)(2,1)S(1)} %collective-permute-done.32.refs_2_, ...), custom_call_target="tpu_custom_call" | custom-call | flops 1887436800 | bytes 14000000 | tf_op jit(solution)/shard_map/expert_grad/pallas_call | solution.py:546
  144.0 2.3 %collective-permute-done.44.refs_1_ = bf16[48,2432]{1,0:T(8,128)(2,1)S(1)} collective-permute-done((bf16[48,2432]{1,0:T(8,128)(2,1)S(1)}, bf16[48,2432]{1,0:T(8,128)(2,1)S(1)}, u32[]{:S(2)}, u32[]{:S(2)}) %collective-permute-start.44) | collective-permute-done | bytes 233504 | tf_op jit(solution)/shard_map/ppermute | solution.py:26
  146.4 2.5 %collective-permute-start.46 = (bf16[96,768]{1,0:T(8,128)(2,1)S(1)}, bf16[96,768]{1,0:T(8,128)(2,1)S(1)}, u32[]{:S(2)}, u32[]{:S(2)}) collective-permute-start(bf16[96,768]{1,0:T(8,128)(2,1)S(1)} %total_sum.6.head_ref), channel_id=1, source_target_pairs={{0,24},{8,16},{16,8},{24,0},{1,25},{9,17},{17,9},{25,1},{2,26},{10... | collective-permute-start | bytes 442376 | tf_op jit(solution)/shard_map/ppermute | solution.py:26
  149.0 7.9 %collective-permute-done.46.head_other = bf16[96,768]{1,0:T(8,128)(2,1)S(1)} collective-permute-done((bf16[96,768]{1,0:T(8,128)(2,1)S(1)}, bf16[96,768]{1,0:T(8,128)(2,1)S(1)}, u32[]{:S(2)}, u32[]{:S(2)}) %collective-permute-start.46) | collective-permute-done | bytes 147488 | tf_op jit(solution)/shard_map/ppermute | solution.py:26
  156.9 1.7 %shares.1 = (f32[96,2304]{1,0:T(8,128)}, f32[96,768]{1,0:T(8,128)}, f32[4,96]{1,0:T(4,128)}, f32[1,96]{1,0:T(1,128)}, f32[1,96]{1,0:T(1,128)}) custom-call(s32[18]{0:T(128)S(1)} %pad_add_fusion.order_ref, bf16[96,768]{1,0:T(8,128)(2,1)S(1)} %total_sum.6.head_ref, bf16[96,768]{1,0:T(8,128)(2,1)S(1)} %collective-permute-done.46.head_other, ...), custom_call_target="tpu_custom_call" | custom-call | flops 1000000 | bytes 1000000 | tf_op jit(solution)/shard_map/shares/pallas_call | solution.py:146
  (112 shorter events, 44.0 us)
Async XLA Ops:
  3.9 8.1 %collective-permute-start = (bf16[64,768]{1,0:T(8,128)(2,1)S(1)}, bf16[64,768]{1,0:T(8,128)(2,1)S(1)}, u32[]{:S(2)}, u32[]{:S(2)}) collective-permute-start(bf16[64,768]{1,0:T(8,128)(2,1)S(1)} %get-tuple-element.108.a0.refs_0_), channel_id=1, source_target_pairs={{0,2},{1,3},{2,0},{3,1},{4,6},{5,7},{6,4},{7,5},{8,10},{9,11},{10,... | collective-permute-start | bytes 294920 | tf_op jit(solution)/shard_map/ppermute | solution.py:26
  8.4 7.7 %collective-permute-start.4 = (bf16[48,2304]{1,0:T(8,128)(2,1)S(1)}, bf16[48,2304]{1,0:T(8,128)(2,1)S(1)}, u32[]{:S(2)}, u32[]{:S(2)}) collective-permute-start(bf16[48,2304]{1,0:T(8,128)(2,1)S(1)} %get-tuple-element.107.a0.refs_0_), channel_id=1, source_target_pairs={{0,2},{1,3},{2,0},{3,1},{4,6},{5,7},{6,4},{7,5},{8,10},{9,11},{10,... | collective-permute-start | bytes 663560 | tf_op jit(solution)/shard_map/ppermute | solution.py:26
  9.0 8.4 %collective-permute-start.5 = (bf16[48,2304]{1,0:T(8,128)(2,1)S(1)}, bf16[48,2304]{1,0:T(8,128)(2,1)S(1)}, u32[]{:S(2)}, u32[]{:S(2)}) collective-permute-start(bf16[48,2304]{1,0:T(8,128)(2,1)S(1)} %get-tuple-element.114.b0.refs_1_), channel_id=1, source_target_pairs={{0,4},{1,5},{2,6},{3,7},{4,0},{5,1},{6,2},{7,3},{8,12},{9,13},{10,... | collective-permute-start | bytes 663560 | tf_op jit(solution)/shard_map/ppermute | solution.py:26
  12.0 8.2 %collective-permute-start.2 = (bf16[128,768]{1,0:T(8,128)(2,1)S(1)}, bf16[128,768]{1,0:T(8,128)(2,1)S(1)}, u32[]{:S(2)}, u32[]{:S(2)}) collective-permute-start(bf16[128,768]{1,0:T(8,128)(2,1)S(1)} %get-tuple-element.112), channel_id=1, source_target_pairs={{0,4},{1,5},{2,6},{3,7},{4,0},{5,1},{6,2},{7,3},{8,12},{9,13},{10,... | collective-permute-start | bytes 589832 | tf_op jit(solution)/shard_map/ppermute | solution.py:26
  20.3 12.6 %collective-permute-start.12 = (bf16[96,2304]{1,0:T(8,128)(2,1)S(1)}, bf16[96,2304]{1,0:T(8,128)(2,1)S(1)}, u32[]{:S(2)}, u32[]{:S(2)}) collective-permute-start(bf16[96,2304]{1,0:T(8,128)(2,1)S(1)} %get-tuple-element.117), channel_id=1, source_target_pairs={{0,4},{1,5},{2,6},{3,7},{4,0},{5,1},{6,2},{7,3},{8,12},{9,13},{10,... | collective-permute-start | bytes 1327112 | tf_op jit(solution)/shard_map/ppermute | solution.py:26
  21.3 11.6 %collective-permute-start.13 = (bf16[96,2304]{1,0:T(8,128)(2,1)S(1)}, bf16[96,2304]{1,0:T(8,128)(2,1)S(1)}, u32[]{:S(2)}, u32[]{:S(2)}) collective-permute-start(bf16[96,2304]{1,0:T(8,128)(2,1)S(1)} %get-tuple-element.118), channel_id=1, source_target_pairs={{0,2},{1,3},{2,0},{3,1},{4,6},{5,7},{6,4},{7,5},{8,10},{9,11},{10,... | collective-permute-start | bytes 1327112 | tf_op jit(solution)/shard_map/ppermute | solution.py:26
  26.2 7.7 %collective-permute-start.14 = (bf16[48,2304]{1,0:T(8,128)(2,1)S(1)}, bf16[48,2304]{1,0:T(8,128)(2,1)S(1)}, u32[]{:S(2)}, u32[]{:S(2)}) collective-permute-start(bf16[48,2304]{1,0:T(8,128)(2,1)S(1)} %get-tuple-element.107.a0.refs_0_), channel_id=1, source_target_pairs={{0,1},{1,0},{2,3},{3,2},{4,5},{5,4},{6,7},{7,6},{8,9},{9,8},{10,11... | collective-permute-start | bytes 663560 | tf_op jit(solution)/shard_map/ppermute | solution.py:26
  61.4 7.2 %collective-permute-start.28 = (bf16[8,1536]{1,0:T(8,128)(2,1)S(1)}, bf16[8,1536]{1,0:T(8,128)(2,1)S(1)}, u32[]{:S(2)}, u32[]{:S(2)}) collective-permute-start(bf16[8,1536]{1,0:T(8,128)(2,1)S(1)} %get-tuple-element.138), channel_id=1, source_target_pairs={{0,2},{1,3},{2,0},{3,1},{4,6},{5,7},{6,4},{7,5},{8,10},{9,11},{10,... | collective-permute-start | bytes 73736 | tf_op jit(solution)/shard_map/ppermute | solution.py:26
  62.2 7.1 %collective-permute-start.29 = (bf16[8,1536]{1,0:T(8,128)(2,1)S(1)}, bf16[8,1536]{1,0:T(8,128)(2,1)S(1)}, u32[]{:S(2)}, u32[]{:S(2)}) collective-permute-start(bf16[8,1536]{1,0:T(8,128)(2,1)S(1)} %get-tuple-element.139), channel_id=1, source_target_pairs={{0,4},{1,5},{2,6},{3,7},{4,0},{5,1},{6,2},{7,3},{8,12},{9,13},{10,... | collective-permute-start | bytes 73736 | tf_op jit(solution)/shard_map/ppermute | solution.py:26
  63.5 5.8 %collective-permute-start.30 = (bf16[8,1536]{1,0:T(8,128)(2,1)S(1)}, bf16[8,1536]{1,0:T(8,128)(2,1)S(1)}, u32[]{:S(2)}, u32[]{:S(2)}) collective-permute-start(bf16[8,1536]{1,0:T(8,128)(2,1)S(1)} %get-tuple-element.140), channel_id=1, source_target_pairs={{0,6},{1,7},{2,4},{3,5},{4,2},{5,3},{6,0},{7,1},{8,14},{9,15},{10,... | collective-permute-start | bytes 73736 | tf_op jit(solution)/shard_map/ppermute | solution.py:26
  65.0 13.7 %collective-permute-start.33 = (bf16[48,1536]{1,0:T(8,128)(2,1)S(1)}, bf16[48,1536]{1,0:T(8,128)(2,1)S(1)}, u32[]{:S(2)}, u32[]{:S(2)}) collective-permute-start(bf16[48,1536]{1,0:T(8,128)(2,1)S(1)} %get-tuple-element.188.refs_0_), channel_id=1, source_target_pairs={{0,24},{8,16},{16,8},{24,0},{1,25},{9,17},{17,9},{25,1},{2,26},{10... | collective-permute-start | bytes 442376 | tf_op jit(solution)/shard_map/ppermute | solution.py:26
  68.6 12.0 %collective-permute-start.32 = (bf16[48,1536]{1,0:T(8,128)(2,1)S(1)}, bf16[48,1536]{1,0:T(8,128)(2,1)S(1)}, u32[]{:S(2)}, u32[]{:S(2)}) collective-permute-start(bf16[48,1536]{1,0:T(8,128)(2,1)S(1)} %get-tuple-element.188.refs_0_), channel_id=1, source_target_pairs={{0,16},{8,24},{16,0},{24,8},{1,17},{9,25},{17,1},{25,9},{2,18},{10... | collective-permute-start | bytes 442376 | tf_op jit(solution)/shard_map/ppermute | solution.py:26
  68.6 12.0 %collective-permute-start.31 = (bf16[48,1536]{1,0:T(8,128)(2,1)S(1)}, bf16[48,1536]{1,0:T(8,128)(2,1)S(1)}, u32[]{:S(2)}, u32[]{:S(2)}) collective-permute-start(bf16[48,1536]{1,0:T(8,128)(2,1)S(1)} %get-tuple-element.188.refs_0_), channel_id=1, source_target_pairs={{0,8},{8,0},{16,24},{24,16},{1,9},{9,1},{17,25},{25,17},{2,10},{10... | collective-permute-start | bytes 442376 | tf_op jit(solution)/shard_map/ppermute | solution.py:26
  100.9 16.5 %collective-permute-start.35 = (bf16[96,2432]{1,0:T(8,128)(2,1)S(1)}, bf16[96,2432]{1,0:T(8,128)(2,1)S(1)}, u32[]{:S(2)}, u32[]{:S(2)}) collective-permute-start(bf16[96,2432]{1,0:T(8,128)(2,1)S(1)} %get-tuple-element.154), channel_id=1, source_target_pairs={{0,2},{1,3},{2,0},{3,1},{4,6},{5,7},{6,4},{7,5},{8,10},{9,11},{10,... | collective-permute-start | bytes 1400840 | tf_op jit(solution)/shard_map/ppermute | solution.py:26
  101.7 21.8 %collective-permute-start.36 = (bf16[96,2432]{1,0:T(8,128)(2,1)S(1)}, bf16[96,2432]{1,0:T(8,128)(2,1)S(1)}, u32[]{:S(2)}, u32[]{:S(2)}) collective-permute-start(bf16[96,2432]{1,0:T(8,128)(2,1)S(1)} %get-tuple-element.155), channel_id=1, source_target_pairs={{0,4},{1,5},{2,6},{3,7},{4,0},{5,1},{6,2},{7,3},{8,12},{9,13},{10,... | collective-permute-start | bytes 1400840 | tf_op jit(solution)/shard_map/ppermute | solution.py:26
  103.0 21.9 %collective-permute-start.37 = (bf16[96,2432]{1,0:T(8,128)(2,1)S(1)}, bf16[96,2432]{1,0:T(8,128)(2,1)S(1)}, u32[]{:S(2)}, u32[]{:S(2)}) collective-permute-start(bf16[96,2432]{1,0:T(8,128)(2,1)S(1)} %get-tuple-element.156), channel_id=1, source_target_pairs={{0,6},{1,7},{2,4},{3,5},{4,2},{5,3},{6,0},{7,1},{8,14},{9,15},{10,... | collective-permute-start | bytes 1400840 | tf_op jit(solution)/shard_map/ppermute | solution.py:26
  115.3 18.7 %collective-permute-start.40 = (bf16[96,768]{1,0:T(8,128)(2,1)S(1)}, bf16[96,768]{1,0:T(8,128)(2,1)S(1)}, u32[]{:S(2)}, u32[]{:S(2)}) collective-permute-start(bf16[96,768]{1,0:T(8,128)(2,1)S(1)} %get-tuple-element.169), channel_id=1, source_target_pairs={{0,2},{1,3},{2,0},{3,1},{4,6},{5,7},{6,4},{7,5},{8,10},{9,11},{10,... | collective-permute-start | bytes 442376 | tf_op jit(solution)/shard_map/ppermute | solution.py:26
  116.2 17.8 %collective-permute-start.41 = (bf16[96,768]{1,0:T(8,128)(2,1)S(1)}, bf16[96,768]{1,0:T(8,128)(2,1)S(1)}, u32[]{:S(2)}, u32[]{:S(2)}) collective-permute-start(bf16[96,768]{1,0:T(8,128)(2,1)S(1)} %get-tuple-element.170), channel_id=1, source_target_pairs={{0,4},{1,5},{2,6},{3,7},{4,0},{5,1},{6,2},{7,3},{8,12},{9,13},{10,... | collective-permute-start | bytes 442376 | tf_op jit(solution)/shard_map/ppermute | solution.py:26
  117.4 16.6 %collective-permute-start.42 = (bf16[96,768]{1,0:T(8,128)(2,1)S(1)}, bf16[96,768]{1,0:T(8,128)(2,1)S(1)}, u32[]{:S(2)}, u32[]{:S(2)}) collective-permute-start(bf16[96,768]{1,0:T(8,128)(2,1)S(1)} %get-tuple-element.171), channel_id=1, source_target_pairs={{0,6},{1,7},{2,4},{3,5},{4,2},{5,3},{6,0},{7,1},{8,14},{9,15},{10,... | collective-permute-start | bytes 442376 | tf_op jit(solution)/shard_map/ppermute | solution.py:26
  125.8 8.2 %collective-permute-start.43 = (bf16[48,2432]{1,0:T(8,128)(2,1)S(1)}, bf16[48,2432]{1,0:T(8,128)(2,1)S(1)}, u32[]{:S(2)}, u32[]{:S(2)}) collective-permute-start(bf16[48,2432]{1,0:T(8,128)(2,1)S(1)} %get-tuple-element.180), channel_id=1, source_target_pairs={{0,8},{8,0},{16,24},{24,16},{1,9},{9,1},{17,25},{25,17},{2,10},{10... | collective-permute-start | bytes 700424 | tf_op jit(solution)/shard_map/ppermute | solution.py:26
  134.2 12.1 %collective-permute-start.44 = (bf16[48,2432]{1,0:T(8,128)(2,1)S(1)}, bf16[48,2432]{1,0:T(8,128)(2,1)S(1)}, u32[]{:S(2)}, u32[]{:S(2)}) collective-permute-start(bf16[48,2432]{1,0:T(8,128)(2,1)S(1)} %total_sum.4.refs_0_), channel_id=1, source_target_pairs={{0,16},{8,24},{16,0},{24,8},{1,17},{9,25},{17,1},{25,9},{2,18},{10... | collective-permute-start | bytes 700424 | tf_op jit(solution)/shard_map/ppermute | solution.py:26
  137.0 6.9 %collective-permute-start.45 = (bf16[96,768]{1,0:T(8,128)(2,1)S(1)}, bf16[96,768]{1,0:T(8,128)(2,1)S(1)}, u32[]{:S(2)}, u32[]{:S(2)}) collective-permute-start(bf16[96,768]{1,0:T(8,128)(2,1)S(1)} %total_sum.5.refs_0_), channel_id=1, source_target_pairs={{0,8},{8,0},{16,24},{24,16},{1,9},{9,1},{17,25},{25,17},{2,10},{10... | collective-permute-start | bytes 442376 | tf_op jit(solution)/shard_map/ppermute | solution.py:26
  146.3 10.6 %collective-permute-start.47 = (bf16[48,2432]{1,0:T(8,128)(2,1)S(1)}, bf16[48,2432]{1,0:T(8,128)(2,1)S(1)}, u32[]{:S(2)}, u32[]{:S(2)}) collective-permute-start(bf16[48,2432]{1,0:T(8,128)(2,1)S(1)} %total_sum.7.tail_ref), channel_id=1, source_target_pairs={{0,8},{8,0},{16,24},{24,16},{1,9},{9,1},{17,25},{25,17},{2,10},{10... | collective-permute-start | bytes 700424 | tf_op jit(solution)/shard_map/ppermute | solution.py:26
  146.4 10.5 %collective-permute-start.46 = (bf16[96,768]{1,0:T(8,128)(2,1)S(1)}, bf16[96,768]{1,0:T(8,128)(2,1)S(1)}, u32[]{:S(2)}, u32[]{:S(2)}) collective-permute-start(bf16[96,768]{1,0:T(8,128)(2,1)S(1)} %total_sum.6.head_ref), channel_id=1, source_target_pairs={{0,24},{8,16},{16,8},{24,0},{1,25},{9,17},{17,9},{25,1},{2,26},{10... | collective-permute-start | bytes 442376 | tf_op jit(solution)/shard_map/ppermute | solution.py:26
  (31 other events, 143.9 us)

commit v3 on v2

--- a/solution.py
+++ b/solution.py
@@ -835,7 +835,7 @@
     output, att, grad_mixed, grad_out, grad_side = back(
         images, places, experts, order, resid, logits, cot, mixes, w_out, small, summed
     )
-    grad_mixed, far = lax.optimization_barrier((grad_mixed, far))
+    grad_mixed, near = lax.optimization_barrier((grad_mixed, far[:1]))
     grad_joint_tail, keep_tail, give_tail = attend_back(
         images, part, order, joint_tail, prob_tail, grad_mixed, mixed_tail, act, (2, 2), (grad_out, grad_side)
     )
@@ -847,7 +847,7 @@
         images, 0, order, joint_head, prob_head, grad_mixed, mixed_head, act, (2, 4, 4)
     )
     joints, weights = [grad_joint_head, grad_joint_tail], [w_head, w_tail]
-    every = [received] + far
+    every = [received] + near + after(far[1:], grad_joint_tail)
     if direct:
         got = [swap(part, "grp", group, 1) for part in give_head]
         own, others = after((sums[0], others), got)

time: 159 us -> 157 us (0.987)
  waiting for transfers between devices: 40.5 us -> 36.1 us
  starting transfers between devices: 37.8 us -> 40.5 us
    ppermute x48, waiting for transfers between devices: 40.5 us -> 36.1 us  [swap(): lax.ppermute(values, axis, [(place, place ^ bit) for place in range(size)])]
    ppermute x48, starting transfers between devices: 37.8 us -> 40.5 us  [swap(): lax.ppermute(values, axis, [(place, place ^ bit) for place in range(size)])]
  transfers between devices with their start and end apart: 48 -> 48, of which waited for: 24 -> 23; matrix products, arithmetic and copies ran while one was open for 1% -> 1% of each run, Pallas kernels for 25% -> 26%
where the time goes in v3:
time: 157 us
  Pallas kernels  74.6 us (48%)
  starting transfers between devices  40.5 us (26%)
  waiting for transfers between devices  36.1 us (23%)
  local copies, waits for them, and re-layouts  3.7 us (2%)
    pallas_call x19, Pallas kernels, call(): pl.pallas_call(body, in_specs=[SM if x.dtype == jnp.int32 else VM for x i...  67.5 us
    ppermute x48, starting transfers between devices, swap(): lax.ppermute(values, axis, [(place, place ^ bit) for place in range(size)])  40.5 us
    ppermute x48, waiting for transfers between devices, swap(): lax.ppermute(values, axis, [(place, place ^ bit) for place in range(size)])  36.1 us
    pallas_call x1, Pallas kernels, expert_grad(): pl.pallas_call(functools.partial(expert_grad_body, len(sources)), grid=(h...  6.66 us
  transfers between devices with their start and end apart: 48, of which 23 were waited for; matrix products, arithmetic and copies ran while one was open for 1% of the time, Pallas kernels for 26%

profile of v3, /device:TPU:0, one launch (start us, length us, event | category | flops | bytes accessed | tf_op | source)
XLA Modules:
  0.0 156.7 jit_solution(3393932115507980325)
XLA Ops:
  3.9 3.0 %collective-permute-start = (bf16[64,768]{1,0:T(8,128)(2,1)S(1)}, bf16[64,768]{1,0:T(8,128)(2,1)S(1)}, u32[]{:S(2)}, u32[]{:S(2)}) collective-permute-start(bf16[64,768]{1,0:T(8,128)(2,1)S(1)} %get-tuple-element.108.a0.refs_0_), channel_id=1, source_target_pairs={{0,2},{1,3},{2,0},{3,1},{4,6},{5,7},{6,4},{7,5},{8,10},{9,11},{10,... | collective-permute-start | bytes 294920 | tf_op jit(solution)/shard_map/ppermute | solution.py:26
  9.0 1.6 %pad.11 = bf16[6,208,768]{2,1,0:T(8,128)(2,1)S(1)} pad(bf16[6,197,768]{2,1,0:T(8,128)(2,1)} %param.9, bf16[]{:T(256)} %constant.62.clone.1), padding=0_0x0_11x0_0 | pad | bytes 3732482 | tf_op jit(solution)/shard_map/jit(_pad)/pad | solution.py:783
  12.0 1.7 %collective-permute-start.2 = (bf16[128,768]{1,0:T(8,128)(2,1)S(1)}, bf16[128,768]{1,0:T(8,128)(2,1)S(1)}, u32[]{:S(2)}, u32[]{:S(2)}) collective-permute-start(bf16[128,768]{1,0:T(8,128)(2,1)S(1)} %get-tuple-element.112), channel_id=1, source_target_pairs={{0,4},{1,5},{2,6},{3,7},{4,0},{5,1},{6,2},{7,3},{8,12},{9,13},{10,... | collective-permute-start | bytes 589832 | tf_op jit(solution)/shard_map/ppermute | solution.py:26
  14.4 1.7 %collective-permute-done.4.a1.refs_2_ = bf16[48,2304]{1,0:T(8,128)(2,1)S(1)} collective-permute-done((bf16[48,2304]{1,0:T(8,128)(2,1)S(1)}, bf16[48,2304]{1,0:T(8,128)(2,1)S(1)}, u32[]{:S(2)}, u32[]{:S(2)}) %collective-permute-start.4) | collective-permute-done | bytes 221216 | tf_op jit(solution)/shard_map/ppermute | solution.py:26
  17.3 1.5 collective-permute-done.3.refs_5_
  26.4 6.5 %attend.2 = (bf16[1248,768]{1,0:T(8,128)(2,1)S(1)}, f32[16,768]{1,0:T(8,128)S(1)}, bf16[768,768]{1,0:T(8,128)(2,1)S(1)}, bf16[1248,768]{1,0:T(8,128)(2,1)S(1)}, ...) custom-call(s32[18]{0:T(128)S(1)} %pad_add_fusion.order_ref, bf16[1248,768]{1,0:T(8,128)(2,1)S(1)} %bitcast.14, ...), custom_call_target="tpu_custom_call" | custom-call | flops 1 | bytes 1000000 | tf_op jit(solution)/shard_map/attend/pallas_call | solution.py:146
  36.3 9.1 %attend.3 = (bf16[768,768]{1,0:T(8,128)(2,1)S(1)}, bf16[768,1536]{1,0:T(8,128)(2,1)S(1)}, bf16[1248,1536]{1,0:T(8,128)(2,1)S(1)}, bf16[48,208,208]{2,1,0:T(8,128)(2,1)S(1)}, bf16[1248,512]{1,0:T(8,128)(2,1)S(1)}) custom-call(s32[18]{0:T(128)S(1)} %pad_add_fusion.order_ref, bf16[1248,768]{1,0:T(8,128)(2,1)S(1)} %get-tuple-element.123.source_ref.act_ref, ...), custom_call_target="tpu_custom_call" | custom-call | flops 5888802816 | bytes 1000000 | tf_op jit(solution)/shard_map/attend/pallas_call | solution.py:146
  45.5 4.1 %route.1 = (f32[1248,768]{1,0:T(8,128)S(1)}, f32[96,208]{1,0:T(8,128)S(1)}, bf16[8,1536]{1,0:T(8,128)(2,1)S(1)}, bf16[8,1536]{1,0:T(8,128)(2,1)S(1)}, bf16[8,153...) custom-call(s32[18]{0:T(128)S(1)} %pad_add_fusion.order_ref, bf16[1248,768]{1,0:T(8,128)(2,1)S(1)} %bitcast.15, ...), custom_call_target="tpu_custom_call" | custom-call | flops 2944401408 | bytes 1000000 | tf_op jit(solution)/shard_map/route/pallas_call | solution.py:146
  54.3 2.0 %collective-permute-done.22.refs_3_ = bf16[8,1536]{1,0:T(8,128)(2,1)S(1)} collective-permute-done((bf16[8,1536]{1,0:T(8,128)(2,1)S(1)}, bf16[8,1536]{1,0:T(8,128)(2,1)S(1)}, u32[]{:S(2)}, u32[]{:S(2)}) %collective-permute-start.22) | collective-permute-done | bytes 24608 | tf_op jit(solution)/shard_map/ppermute | solution.py:26
  57.6 2.4 %expert.1 = (bf16[48,1536]{1,0:T(8,128)(2,1)S(1)}, bf16[32,1536]{1,0:T(8,128)(2,1)S(1)}, bf16[32,1536]{1,0:T(8,128)(2,1)S(1)}) custom-call(bf16[768,1536]{1,0:T(8,128)(2,1)S(1)} %bitcast.17, bf16[1536,768]{1,0:T(8,128)(2,1)S(1)} %bitcast.19, bf16[8,1536]{1,0:T(8,128)(2,1)S(1)} %get-tuple-element.131.refs_0_, ...), custom_call_target="tpu_custom_call" | custom-call | flops 1000000000 | bytes 1000000 | tf_op jit(solution)/shard_map/expert/pallas_call | solution.py:146
  65.0 1.6 %collective-permute-start.31 = (bf16[48,1536]{1,0:T(8,128)(2,1)S(1)}, bf16[48,1536]{1,0:T(8,128)(2,1)S(1)}, u32[]{:S(2)}, u32[]{:S(2)}) collective-permute-start(bf16[48,1536]{1,0:T(8,128)(2,1)S(1)} %get-tuple-element.188.refs_0_), channel_id=1, source_target_pairs={{0,8},{8,0},{16,24},{24,16},{1,9},{9,1},{17,25},{25,17},{2,10},{10... | collective-permute-start | bytes 442376 | tf_op jit(solution)/shard_map/ppermute | solution.py:26
  66.5 1.7 %collective-permute-done.30.refs_3_ = bf16[8,1536]{1,0:T(8,128)(2,1)S(1)} collective-permute-done((bf16[8,1536]{1,0:T(8,128)(2,1)S(1)}, bf16[8,1536]{1,0:T(8,128)(2,1)S(1)}, u32[]{:S(2)}, u32[]{:S(2)}) %collective-permute-start.30) | collective-permute-done | bytes 24608 | tf_op jit(solution)/shard_map/ppermute | solution.py:26
  68.2 9.3 %back.1 = (bf16[6,197,768]{2,1,0:T(8,128)(2,1)}, bf16[1248,768]{1,0:T(8,128)(2,1)S(1)}, bf16[1248,768]{1,0:T(8,128)(2,1)S(1)}, bf16[768,768]{1,0:T(8,128)(2,1)S(1)}, bf16[768,128]{1,0:T(8,128)(2,1)S(1)}) custom-call(s32[18]{0:T(128)S(1)} %pad_add_fusion.order_ref, f32[1248,768]{1,0:T(8,128)S(1)} %get-tuple-element.129.resid_ref, ...), custom_call_target="tpu_custom_call" | custom-call | flops 5888802816 | bytes 1000000 | tf_op jit(solution)/shard_map/back/pallas_call | solution.py:146
  77.5 16.0 %attend_back.2 = (bf16[1248,1536]{1,0:T(8,128)(2,1)S(1)}, bf16[384,2432]{1,0:T(8,128)(2,1)S(1)}, bf16[384,2432]{1,0:T(8,128)(2,1)S(1)}) custom-call(s32[18]{0:T(128)S(1)} %pad_add_fusion.order_ref, bf16[1248,1536]{1,0:T(8,128)(2,1)S(1)} %get-tuple-element.143.joint_ref, bf16[48,208,208]{2,1,0:T(8,128)(2,1)S(1)} %get-tuple-element.144.prob_ref, ...), custom_call_target="tpu_custom_call" | custom-call | flops 11777605632 | bytes 1000000 | tf_op jit(solution)/shard_map/attend_back/pallas_call | solution.py:146
  93.7 2.7 %collective-permute-start.38 = (bf16[48,1536]{1,0:T(8,128)(2,1)S(1)}, bf16[48,1536]{1,0:T(8,128)(2,1)S(1)}, u32[]{:S(2)}, u32[]{:S(2)}) collective-permute-start(bf16[48,1536]{1,0:T(8,128)(2,1)S(1)} %get-tuple-element.188.refs_0_), channel_id=1, source_target_pairs={{0,16},{8,24},{16,0},{24,8},{1,17},{9,25},{17,1},{25,9},{2,18},{10... | collective-permute-start | bytes 442376 | tf_op jit(solution)/shard_map/ppermute | solution.py:26
  101.7 8.6 %attend_back.3 = (bf16[1248,768]{1,0:T(8,128)(2,1)S(1)}, bf16[384,768]{1,0:T(8,128)(2,1)S(1)}, bf16[192,768]{1,0:T(8,128)(2,1)S(1)}, bf16[192,768]{1,0:T(8,128)(2,1)S(1)}) custom-call(s32[18]{0:T(128)S(1)} %pad_add_fusion.order_ref, bf16[1248,768]{1,0:T(8,128)(2,1)S(1)} %get-tuple-element.157.joint_ref, ...), custom_call_target="tpu_custom_call" | custom-call | flops 5888802816 | bytes 1000000 | tf_op jit(solution)/shard_map/attend_back/pallas_call | solution.py:146
  116.1 5.0 %collective-permute-done.34.refs_2_ = bf16[96,2432]{1,0:T(8,128)(2,1)S(1)} collective-permute-done((bf16[96,2432]{1,0:T(8,128)(2,1)S(1)}, bf16[96,2432]{1,0:T(8,128)(2,1)S(1)}, u32[]{:S(2)}, u32[]{:S(2)}) %collective-permute-start.34) | collective-permute-done | bytes 466976 | tf_op jit(solution)/shard_map/ppermute | solution.py:26
  124.4 7.8 %finish.1 = bf16[6,197,768]{2,1,0:T(8,128)(2,1)} custom-call(bf16[1248,768]{1,0:T(8,128)(2,1)S(1)} %bitcast.16, bf16[1248,768]{1,0:T(8,128)(2,1)S(1)} %get-tuple-element.172.att_ref, bf16[1248,768]{1,0:T(8,128)(2,1)S(1)} %get-tuple-element.173.j0, bf16[1248,1536]{1,0:T(8,128)(2,1)S(1)} %get-tuple-element.174.j1, bf16[768,768]{1,0:T(8,128)(2,1)S(1)} %get-tuple-element.175.s0, ...), custom_call_target="tpu_custom_call" | custom-call | flops 4416602112 | bytes 1000000 | tf_op jit(solution)/shard_map/finish/pallas_call | solution.py:146
  132.4 2.6 %collective-permute-start.44 = (bf16[48,2432]{1,0:T(8,128)(2,1)S(1)}, bf16[48,2432]{1,0:T(8,128)(2,1)S(1)}, u32[]{:S(2)}, u32[]{:S(2)}) collective-permute-start(bf16[48,2432]{1,0:T(8,128)(2,1)S(1)} %total_sum.4.refs_0_), channel_id=1, source_target_pairs={{0,16},{8,24},{16,0},{24,8},{1,17},{9,25},{17,1},{25,9},{2,18},{10... | collective-permute-start | bytes 700424 | tf_op jit(solution)/shard_map/ppermute | solution.py:26
  135.5 6.7 %expert_grad.1 = (f32[768,1536]{1,0:T(8,128)}, f32[1536,768]{1,0:T(8,128)}) custom-call(bf16[48,1536]{1,0:T(8,128)(2,1)S(1)} %get-tuple-element.188.refs_0_, bf16[48,1536]{1,0:T(8,128)(2,1)S(1)} %collective-permute-done.31.refs_1_, bf16[48,1536]{1,0:T(8,128)(2,1)S(1)} %collective-permute-done.38.refs_2_, ...), custom_call_target="tpu_custom_call" | custom-call | flops 1887436800 | bytes 14000000 | tf_op jit(solution)/shard_map/expert_grad/pallas_call | solution.py:546
  142.1 2.0 %collective-permute-done.44.refs_1_ = bf16[48,2432]{1,0:T(8,128)(2,1)S(1)} collective-permute-done((bf16[48,2432]{1,0:T(8,128)(2,1)S(1)}, bf16[48,2432]{1,0:T(8,128)(2,1)S(1)}, u32[]{:S(2)}, u32[]{:S(2)}) %collective-permute-start.44) | collective-permute-done | bytes 233504 | tf_op jit(solution)/shard_map/ppermute | solution.py:26
  144.4 2.6 %collective-permute-start.46 = (bf16[96,768]{1,0:T(8,128)(2,1)S(1)}, bf16[96,768]{1,0:T(8,128)(2,1)S(1)}, u32[]{:S(2)}, u32[]{:S(2)}) collective-permute-start(bf16[96,768]{1,0:T(8,128)(2,1)S(1)} %total_sum.6.head_ref), channel_id=1, source_target_pairs={{0,24},{8,16},{16,8},{24,0},{1,25},{9,17},{17,9},{25,1},{2,26},{10... | collective-permute-start | bytes 442376 | tf_op jit(solution)/shard_map/ppermute | solution.py:26
  147.0 7.9 %collective-permute-done.46.head_other = bf16[96,768]{1,0:T(8,128)(2,1)S(1)} collective-permute-done((bf16[96,768]{1,0:T(8,128)(2,1)S(1)}, bf16[96,768]{1,0:T(8,128)(2,1)S(1)}, u32[]{:S(2)}, u32[]{:S(2)}) %collective-permute-start.46) | collective-permute-done | bytes 147488 | tf_op jit(solution)/shard_map/ppermute | solution.py:26
  155.0 1.7 %shares.1 = (f32[96,2304]{1,0:T(8,128)}, f32[96,768]{1,0:T(8,128)}, f32[4,96]{1,0:T(4,128)}, f32[1,96]{1,0:T(1,128)}, f32[1,96]{1,0:T(1,128)}) custom-call(s32[18]{0:T(128)S(1)} %pad_add_fusion.order_ref, bf16[96,768]{1,0:T(8,128)(2,1)S(1)} %total_sum.6.head_ref, bf16[96,768]{1,0:T(8,128)(2,1)S(1)} %collective-permute-done.46.head_other, ...), custom_call_target="tpu_custom_call" | custom-call | flops 1000000 | bytes 1000000 | tf_op jit(solution)/shard_map/shares/pallas_call | solution.py:146
  (112 shorter events, 45.7 us)
Async XLA Ops:
  3.9 8.1 %collective-permute-start = (bf16[64,768]{1,0:T(8,128)(2,1)S(1)}, bf16[64,768]{1,0:T(8,128)(2,1)S(1)}, u32[]{:S(2)}, u32[]{:S(2)}) collective-permute-start(bf16[64,768]{1,0:T(8,128)(2,1)S(1)} %get-tuple-element.108.a0.refs_0_), channel_id=1, source_target_pairs={{0,2},{1,3},{2,0},{3,1},{4,6},{5,7},{6,4},{7,5},{8,10},{9,11},{10,... | collective-permute-start | bytes 294920 | tf_op jit(solution)/shard_map/ppermute | solution.py:26
  6.9 5.1 %collective-permute-start.1 = (bf16[48,768]{1,0:T(8,128)(2,1)S(1)}, bf16[48,768]{1,0:T(8,128)(2,1)S(1)}, u32[]{:S(2)}, u32[]{:S(2)}) collective-permute-start(bf16[48,768]{1,0:T(8,128)(2,1)S(1)} %get-tuple-element.109.b0.refs_1_), channel_id=1, source_target_pairs={{0,4},{1,5},{2,6},{3,7},{4,0},{5,1},{6,2},{7,3},{8,12},{9,13},{10,... | collective-permute-start | bytes 221192 | tf_op jit(solution)/shard_map/ppermute | solution.py:26
  8.4 7.7 %collective-permute-start.4 = (bf16[48,2304]{1,0:T(8,128)(2,1)S(1)}, bf16[48,2304]{1,0:T(8,128)(2,1)S(1)}, u32[]{:S(2)}, u32[]{:S(2)}) collective-permute-start(bf16[48,2304]{1,0:T(8,128)(2,1)S(1)} %get-tuple-element.107.a0.refs_0_), channel_id=1, source_target_pairs={{0,2},{1,3},{2,0},{3,1},{4,6},{5,7},{6,4},{7,5},{8,10},{9,11},{10,... | collective-permute-start | bytes 663560 | tf_op jit(solution)/shard_map/ppermute | solution.py:26
  9.0 8.4 %collective-permute-start.5 = (bf16[48,2304]{1,0:T(8,128)(2,1)S(1)}, bf16[48,2304]{1,0:T(8,128)(2,1)S(1)}, u32[]{:S(2)}, u32[]{:S(2)}) collective-permute-start(bf16[48,2304]{1,0:T(8,128)(2,1)S(1)} %get-tuple-element.114.b0.refs_1_), channel_id=1, source_target_pairs={{0,4},{1,5},{2,6},{3,7},{4,0},{5,1},{6,2},{7,3},{8,12},{9,13},{10,... | collective-permute-start | bytes 663560 | tf_op jit(solution)/shard_map/ppermute | solution.py:26
  12.0 8.2 %collective-permute-start.2 = (bf16[128,768]{1,0:T(8,128)(2,1)S(1)}, bf16[128,768]{1,0:T(8,128)(2,1)S(1)}, u32[]{:S(2)}, u32[]{:S(2)}) collective-permute-start(bf16[128,768]{1,0:T(8,128)(2,1)S(1)} %get-tuple-element.112), channel_id=1, source_target_pairs={{0,4},{1,5},{2,6},{3,7},{4,0},{5,1},{6,2},{7,3},{8,12},{9,13},{10,... | collective-permute-start | bytes 589832 | tf_op jit(solution)/shard_map/ppermute | solution.py:26
  13.7 5.1 %collective-permute-start.3 = (bf16[96,768]{1,0:T(8,128)(2,1)S(1)}, bf16[96,768]{1,0:T(8,128)(2,1)S(1)}, u32[]{:S(2)}, u32[]{:S(2)}) collective-permute-start(bf16[96,768]{1,0:T(8,128)(2,1)S(1)} %get-tuple-element.113), channel_id=1, source_target_pairs={{0,2},{1,3},{2,0},{3,1},{4,6},{5,7},{6,4},{7,5},{8,10},{9,11},{10,... | collective-permute-start | bytes 442376 | tf_op jit(solution)/shard_map/ppermute | solution.py:26
  20.3 12.6 %collective-permute-start.12 = (bf16[96,2304]{1,0:T(8,128)(2,1)S(1)}, bf16[96,2304]{1,0:T(8,128)(2,1)S(1)}, u32[]{:S(2)}, u32[]{:S(2)}) collective-permute-start(bf16[96,2304]{1,0:T(8,128)(2,1)S(1)} %get-tuple-element.117), channel_id=1, source_target_pairs={{0,4},{1,5},{2,6},{3,7},{4,0},{5,1},{6,2},{7,3},{8,12},{9,13},{10,... | collective-permute-start | bytes 1327112 | tf_op jit(solution)/shard_map/ppermute | solution.py:26
  21.3 11.6 %collective-permute-start.13 = (bf16[96,2304]{1,0:T(8,128)(2,1)S(1)}, bf16[96,2304]{1,0:T(8,128)(2,1)S(1)}, u32[]{:S(2)}, u32[]{:S(2)}) collective-permute-start(bf16[96,2304]{1,0:T(8,128)(2,1)S(1)} %get-tuple-element.118), channel_id=1, source_target_pairs={{0,2},{1,3},{2,0},{3,1},{4,6},{5,7},{6,4},{7,5},{8,10},{9,11},{10,... | collective-permute-start | bytes 1327112 | tf_op jit(solution)/shard_map/ppermute | solution.py:26
  26.2 7.7 %collective-permute-start.14 = (bf16[48,2304]{1,0:T(8,128)(2,1)S(1)}, bf16[48,2304]{1,0:T(8,128)(2,1)S(1)}, u32[]{:S(2)}, u32[]{:S(2)}) collective-permute-start(bf16[48,2304]{1,0:T(8,128)(2,1)S(1)} %get-tuple-element.107.a0.refs_0_), channel_id=1, source_target_pairs={{0,1},{1,0},{2,3},{3,2},{4,5},{5,4},{6,7},{7,6},{8,9},{9,8},{10,11... | collective-permute-start | bytes 663560 | tf_op jit(solution)/shard_map/ppermute | solution.py:26
  61.4 5.1 %collective-permute-start.28 = (bf16[8,1536]{1,0:T(8,128)(2,1)S(1)}, bf16[8,1536]{1,0:T(8,128)(2,1)S(1)}, u32[]{:S(2)}, u32[]{:S(2)}) collective-permute-start(bf16[8,1536]{1,0:T(8,128)(2,1)S(1)} %get-tuple-element.138), channel_id=1, source_target_pairs={{0,2},{1,3},{2,0},{3,1},{4,6},{5,7},{6,4},{7,5},{8,10},{9,11},{10,... | collective-permute-start | bytes 73736 | tf_op jit(solution)/shard_map/ppermute | solution.py:26
  65.0 12.6 %collective-permute-start.31 = (bf16[48,1536]{1,0:T(8,128)(2,1)S(1)}, bf16[48,1536]{1,0:T(8,128)(2,1)S(1)}, u32[]{:S(2)}, u32[]{:S(2)}) collective-permute-start(bf16[48,1536]{1,0:T(8,128)(2,1)S(1)} %get-tuple-element.188.refs_0_), channel_id=1, source_target_pairs={{0,8},{8,0},{16,24},{24,16},{1,9},{9,1},{17,25},{25,17},{2,10},{10... | collective-permute-start | bytes 442376 | tf_op jit(solution)/shard_map/ppermute | solution.py:26
  93.7 16.7 %collective-permute-start.38 = (bf16[48,1536]{1,0:T(8,128)(2,1)S(1)}, bf16[48,1536]{1,0:T(8,128)(2,1)S(1)}, u32[]{:S(2)}, u32[]{:S(2)}) collective-permute-start(bf16[48,1536]{1,0:T(8,128)(2,1)S(1)} %get-tuple-element.188.refs_0_), channel_id=1, source_target_pairs={{0,16},{8,24},{16,0},{24,8},{1,17},{9,25},{17,1},{25,9},{2,18},{10... | collective-permute-start | bytes 442376 | tf_op jit(solution)/shard_map/ppermute | solution.py:26
  96.3 14.1 %collective-permute-start.39 = (bf16[48,1536]{1,0:T(8,128)(2,1)S(1)}, bf16[48,1536]{1,0:T(8,128)(2,1)S(1)}, u32[]{:S(2)}, u32[]{:S(2)}) collective-permute-start(bf16[48,1536]{1,0:T(8,128)(2,1)S(1)} %get-tuple-element.188.refs_0_), channel_id=1, source_target_pairs={{0,24},{8,16},{16,8},{24,0},{1,25},{9,17},{17,9},{25,1},{2,26},{10... | collective-permute-start | bytes 442376 | tf_op jit(solution)/shard_map/ppermute | solution.py:26
  98.1 16.5 %collective-permute-start.33 = (bf16[96,2432]{1,0:T(8,128)(2,1)S(1)}, bf16[96,2432]{1,0:T(8,128)(2,1)S(1)}, u32[]{:S(2)}, u32[]{:S(2)}) collective-permute-start(bf16[96,2432]{1,0:T(8,128)(2,1)S(1)} %get-tuple-element.154), channel_id=1, source_target_pairs={{0,2},{1,3},{2,0},{3,1},{4,6},{5,7},{6,4},{7,5},{8,10},{9,11},{10,... | collective-permute-start | bytes 1400840 | tf_op jit(solution)/shard_map/ppermute | solution.py:26
  99.0 22.1 %collective-permute-start.34 = (bf16[96,2432]{1,0:T(8,128)(2,1)S(1)}, bf16[96,2432]{1,0:T(8,128)(2,1)S(1)}, u32[]{:S(2)}, u32[]{:S(2)}) collective-permute-start(bf16[96,2432]{1,0:T(8,128)(2,1)S(1)} %get-tuple-element.155), channel_id=1, source_target_pairs={{0,4},{1,5},{2,6},{3,7},{4,0},{5,1},{6,2},{7,3},{8,12},{9,13},{10,... | collective-permute-start | bytes 1400840 | tf_op jit(solution)/shard_map/ppermute | solution.py:26
  100.2 21.8 %collective-permute-start.35 = (bf16[96,2432]{1,0:T(8,128)(2,1)S(1)}, bf16[96,2432]{1,0:T(8,128)(2,1)S(1)}, u32[]{:S(2)}, u32[]{:S(2)}) collective-permute-start(bf16[96,2432]{1,0:T(8,128)(2,1)S(1)} %get-tuple-element.156), channel_id=1, source_target_pairs={{0,6},{1,7},{2,4},{3,5},{4,2},{5,3},{6,0},{7,1},{8,14},{9,15},{10,... | collective-permute-start | bytes 1400840 | tf_op jit(solution)/shard_map/ppermute | solution.py:26
  112.5 19.7 %collective-permute-start.40 = (bf16[96,768]{1,0:T(8,128)(2,1)S(1)}, bf16[96,768]{1,0:T(8,128)(2,1)S(1)}, u32[]{:S(2)}, u32[]{:S(2)}) collective-permute-start(bf16[96,768]{1,0:T(8,128)(2,1)S(1)} %get-tuple-element.169), channel_id=1, source_target_pairs={{0,2},{1,3},{2,0},{3,1},{4,6},{5,7},{6,4},{7,5},{8,10},{9,11},{10,... | collective-permute-start | bytes 442376 | tf_op jit(solution)/shard_map/ppermute | solution.py:26
  113.5 18.7 %collective-permute-start.41 = (bf16[96,768]{1,0:T(8,128)(2,1)S(1)}, bf16[96,768]{1,0:T(8,128)(2,1)S(1)}, u32[]{:S(2)}, u32[]{:S(2)}) collective-permute-start(bf16[96,768]{1,0:T(8,128)(2,1)S(1)} %get-tuple-element.170), channel_id=1, source_target_pairs={{0,4},{1,5},{2,6},{3,7},{4,0},{5,1},{6,2},{7,3},{8,12},{9,13},{10,... | collective-permute-start | bytes 442376 | tf_op jit(solution)/shard_map/ppermute | solution.py:26
  114.6 17.6 %collective-permute-start.42 = (bf16[96,768]{1,0:T(8,128)(2,1)S(1)}, bf16[96,768]{1,0:T(8,128)(2,1)S(1)}, u32[]{:S(2)}, u32[]{:S(2)}) collective-permute-start(bf16[96,768]{1,0:T(8,128)(2,1)S(1)} %get-tuple-element.171), channel_id=1, source_target_pairs={{0,6},{1,7},{2,4},{3,5},{4,2},{5,3},{6,0},{7,1},{8,14},{9,15},{10,... | collective-permute-start | bytes 442376 | tf_op jit(solution)/shard_map/ppermute | solution.py:26
  123.0 9.2 %collective-permute-start.43 = (bf16[48,2432]{1,0:T(8,128)(2,1)S(1)}, bf16[48,2432]{1,0:T(8,128)(2,1)S(1)}, u32[]{:S(2)}, u32[]{:S(2)}) collective-permute-start(bf16[48,2432]{1,0:T(8,128)(2,1)S(1)} %get-tuple-element.180), channel_id=1, source_target_pairs={{0,8},{8,0},{16,24},{24,16},{1,9},{9,1},{17,25},{25,17},{2,10},{10... | collective-permute-start | bytes 700424 | tf_op jit(solution)/shard_map/ppermute | solution.py:26
  132.4 11.8 %collective-permute-start.44 = (bf16[48,2432]{1,0:T(8,128)(2,1)S(1)}, bf16[48,2432]{1,0:T(8,128)(2,1)S(1)}, u32[]{:S(2)}, u32[]{:S(2)}) collective-permute-start(bf16[48,2432]{1,0:T(8,128)(2,1)S(1)} %total_sum.4.refs_0_), channel_id=1, source_target_pairs={{0,16},{8,24},{16,0},{24,8},{1,17},{9,25},{17,1},{25,9},{2,18},{10... | collective-permute-start | bytes 700424 | tf_op jit(solution)/shard_map/ppermute | solution.py:26
  135.0 7.1 %collective-permute-start.45 = (bf16[96,768]{1,0:T(8,128)(2,1)S(1)}, bf16[96,768]{1,0:T(8,128)(2,1)S(1)}, u32[]{:S(2)}, u32[]{:S(2)}) collective-permute-start(bf16[96,768]{1,0:T(8,128)(2,1)S(1)} %total_sum.5.refs_0_), channel_id=1, source_target_pairs={{0,8},{8,0},{16,24},{24,16},{1,9},{9,1},{17,25},{25,17},{2,10},{10... | collective-permute-start | bytes 442376 | tf_op jit(solution)/shard_map/ppermute | solution.py:26
  144.2 10.7 %collective-permute-start.47 = (bf16[48,2432]{1,0:T(8,128)(2,1)S(1)}, bf16[48,2432]{1,0:T(8,128)(2,1)S(1)}, u32[]{:S(2)}, u32[]{:S(2)}) collective-permute-start(bf16[48,2432]{1,0:T(8,128)(2,1)S(1)} %total_sum.7.tail_ref), channel_id=1, source_target_pairs={{0,8},{8,0},{16,24},{24,16},{1,9},{9,1},{17,25},{25,17},{2,10},{10... | collective-permute-start | bytes 700424 | tf_op jit(solution)/shard_map/ppermute | solution.py:26
  144.4 10.6 %collective-permute-start.46 = (bf16[96,768]{1,0:T(8,128)(2,1)S(1)}, bf16[96,768]{1,0:T(8,128)(2,1)S(1)}, u32[]{:S(2)}, u32[]{:S(2)}) collective-permute-start(bf16[96,768]{1,0:T(8,128)(2,1)S(1)} %total_sum.6.head_ref), channel_id=1, source_target_pairs={{0,24},{8,16},{16,8},{24,0},{1,25},{9,17},{17,9},{25,1},{2,26},{10... | collective-permute-start | bytes 442376 | tf_op jit(solution)/shard_map/ppermute | solution.py:26
  (31 other events, 142.5 us)
